TPU v7x, 32 devices: a whole 2x2x4 slice. The times are simulated.
32 devices in a mesh: gx: 2 (over y), gy: 4 (over x, core), gz: 4 (over z).
Axes of the slice: x: 2, y: 2, z: 4, core: 2. Of those that a mesh axis runs over, the one named last changes fastest.
Arguments:
- features: bfloat16 [2, 16, 128, 256], P('gx', 'gy', 'gz'), may hold values from -6 to 6
- neighbour_code: int32 [2, 16, 128, 64], P('gx', 'gy', 'gz'), may hold values from 0 to 107, as said below
- distance: float32 [2, 16, 128, 64], P('gx', 'gy', 'gz'), may hold values from 0.8 to 4.8
- w_message: bfloat16 [2, 2048, 256], replicated, may hold values from -0.125 to 0.125
- w_update: bfloat16 [2, 256, 256], replicated, may hold values from -0.375 to 0.375
- norm_gain: float32 [2, 256], replicated, may hold values from 0.1 to 1.9
- w_env: bfloat16 [256, 128], replicated, may hold values from -0.375 to 0.375
- w_out: bfloat16 [3, 256], replicated, may hold values from -0.375 to 0.375
- w_first: bfloat16 [8, 128, 1024], P(('gx', 'gy')), may hold values from -0.5 to 0.5
- w_head: bfloat16 [8, 3, 1024], P(('gx', 'gy')), may hold values from -0.75 to 0.75
- flag_ids: int32 [2, 4, 4, 32], P('gx', 'gy', 'gz'), may hold values from 0 to 127, as said below
- flag_owner: int32 [2, 4, 4, 32, 1], P('gx', 'gy', 'gz'), may hold values from 0 to 7; in each aligned block of 32 rows (0 to 31, 32 to 63, ..., all dimensions but the last counted through in order) at most 8 rows name the same one
- flag_count: int32 [2, 4, 4], P('gx', 'gy', 'gz'), may hold values from 24 to 32, as said below
Outputs:
- forces: float32 [3, 2, 16, 128], P(None, 'gx', 'gy', 'gz')
Inputs may be any that keep to these rules, and one draw needn't show every extreme that they name: `neighbour_code`: an atom's 64 codes are distinct and never name the atom itself (code 13 * 4 + its position along the thickness mod 4). `flag_ids`: the 32 indices of one device are distinct. `flag_owner`: of the 32 rows of one device, live or not, at most 8 name the same specialist, and some device has 8 rows naming one. Rows 0 to flag_count - 1 of a device are live; some device has all 32 live.
All inputs are finite; a program needn't handle non-finite values.
Results may differ from a plain program's by a relative error of at most 0.0085.
Values may be sent and summed in bfloat16 or wider, within the bound.
A program may use at most 64 MiB of HBM per device.

v0:
```python
import math

import jax
import jax.numpy as jnp
from jax import lax
from jax.sharding import PartitionSpec as P

M = 4
NRB = 8
L = 2


CUTOFF_RADIUS = 5.0
WIDTH_GAMMA = 2.0


def with_halo(cells, sides, width, closed):
    for axis, dim in sides:
        count = lax.axis_size(axis)
        ends = count if closed else count - 1
        head = lax.slice_in_dim(cells, 0, width, axis=dim)
        tail = lax.slice_in_dim(cells, cells.shape[dim] - width, cells.shape[dim], axis=dim)
        cells = jnp.concatenate(
            [
                lax.ppermute(tail, axis, [(i, (i + 1) % count) for i in range(ends)]),
                cells,
                lax.ppermute(head, axis, [((i + 1) % count, i) for i in range(ends)]),
            ],
            axis=dim,
        )
    return cells


def radial(distance):
    cutoff = 0.5 * (jnp.cos(jnp.pi * distance / CUTOFF_RADIUS) + 1.0)
    centres = 0.8 + jnp.arange(NRB).astype(distance.dtype) * (4.0 / (NRB - 1))
    radial_basis = jnp.exp(-WIDTH_GAMMA * (distance[..., None] - centres) ** 2) * cutoff[..., None]
    return (radial_basis.astype(jnp.bfloat16), cutoff)


def neighbour_rows(codes, coord_x, coord_y, coord_z, span_y, span_z):
    offset = codes // M
    within = codes % M
    step_x = offset // 9 - 1
    step_y = offset // 3 % 3 - 1
    step_z = offset % 3 - 1
    return (
        ((coord_x + 1 + step_x) * span_y + (coord_y + 1 + step_y)) * span_z
        + (coord_z // M + 1 + step_z) * M
        + within
    )


def update(state, summed, w_message, w_update, gain):
    message = jnp.dot(summed, w_message, preferred_element_type=jnp.float32)
    active = jax.nn.silu(message).astype(jnp.bfloat16)
    residual = state.astype(jnp.float32) + jnp.dot(
        active, w_update, preferred_element_type=jnp.float32
    )
    inv_rms = lax.rsqrt(jnp.mean(residual * residual, axis=-1, keepdims=True) + 1e-06)
    return (residual * inv_rms * gain).astype(jnp.bfloat16)


def ghosts(values):
    deeper = with_halo(values, (("gz", 2),), M, False)
    return with_halo(deeper, (("gx", 0), ("gy", 1)), 1, True)


def cheap_layer(state, row_index, radial_basis, w_message, w_update, gain):
    feature_width = state.shape[-1]
    flat_rows = ghosts(state).reshape(-1, feature_width)
    atom_count = row_index.shape[0]
    block_size = math.gcd(atom_count, 128)

    def one_block(offset):
        nearby = flat_rows[row_index]
        summed = jnp.einsum(
            "ask,asf->akf", radial_basis, nearby, preferred_element_type=jnp.float32
        )
        return summed.reshape(block_size, -1).astype(jnp.bfloat16)

    starts = jnp.arange(atom_count // block_size, dtype=jnp.int32) * block_size
    summed = lax.map(one_block, starts).reshape(atom_count, -1)
    return update(
        state.reshape(atom_count, feature_width), summed, w_message, w_update, gain
    ).reshape(state.shape)


def specialist(received, live_mark, w_first, w_head):
    sources, item_count = (received.shape[0], received.shape[1])
    env_total = sources * item_count
    block_size = math.gcd(env_total, 16)
    environs = received.reshape(env_total, received.shape[2], received.shape[3])
    flat_live = live_mark.reshape(env_total).astype(jnp.float32) > 0.5

    def run_block(env_piece):
        hidden = jax.nn.silu(
            jnp.einsum("bse,eh->bsh", env_piece, w_first, preferred_element_type=jnp.float32)
        ).astype(jnp.bfloat16)
        pooled = (jnp.sum(hidden, axis=1, dtype=jnp.float32) / hidden.shape[1]).astype(jnp.bfloat16)
        return jnp.einsum("bh,ch->bc", pooled, w_head, preferred_element_type=jnp.float32)

    order = jnp.argsort(jnp.where(flat_live, 0, 1).astype(jnp.int32), stable=True)
    live_total = jnp.sum(flat_live.astype(jnp.int32))
    ordered = environs[order]
    block_count = (live_total + block_size - 1) // block_size

    def step_block(index, gathered):
        offset = index * block_size
        piece = lax.dynamic_slice_in_dim(ordered, offset, block_size, 0)
        return lax.dynamic_update_slice_in_dim(gathered, run_block(piece), offset, 0)

    sorted_results = lax.fori_loop(
        0, block_count, step_block, jnp.zeros((env_total, 3), jnp.float32)
    )
    results = jnp.zeros((env_total, 3), jnp.float32).at[order].set(sorted_results)
    results = results * flat_live[:, None].astype(jnp.float32)
    return results.reshape(sources, item_count, 3)


def per_device(
    features,
    neighbour_code,
    distance,
    w_message,
    w_update,
    norm_gain,
    w_env,
    w_out,
    w_first,
    w_head,
    flag_ids,
    flag_owner,
    flag_count,
):
    cells_x, cells_y, depth, feature_width = features.shape
    atom_count = cells_x * cells_y * depth
    position = jnp.arange(atom_count, dtype=jnp.int32)
    coord_x = position // (cells_y * depth)
    coord_y = position // depth % cells_y
    coord_z = position % depth
    codes = neighbour_code.reshape(atom_count, -1)
    row_index = neighbour_rows(
        codes, coord_x[:, None], coord_y[:, None], coord_z[:, None], cells_y + 2, depth + 2 * M
    )
    radial_basis, cutoff = radial(distance.reshape(atom_count, -1))
    state = features
    for layer_index in range(L):
        state = cheap_layer(
            state,
            row_index,
            radial_basis,
            w_message[layer_index],
            w_update[layer_index],
            norm_gain[layer_index],
        )
    flat_state = state.reshape(atom_count, feature_width)
    projected = jnp.dot(flat_state, w_env, preferred_element_type=jnp.float32).astype(jnp.bfloat16)
    env_width = projected.shape[-1]
    proj_rows = ghosts(projected.reshape(cells_x, cells_y, depth, env_width)).reshape(-1, env_width)
    base_force = jnp.einsum("af,cf->ca", flat_state, w_out, preferred_element_type=jnp.float32)
    local_ids = flag_ids.reshape(-1)
    owner = flag_owner.reshape(-1)
    flag_total = local_ids.shape[0]
    live_rows = jnp.arange(flag_total, dtype=jnp.int32) < flag_count.reshape(())
    nearby = proj_rows[row_index[local_ids]]
    environ = (cutoff[local_ids][..., None] * nearby.astype(jnp.float32)).astype(jnp.bfloat16)
    owner_total = lax.axis_size("gx") * lax.axis_size("gy")
    capacity = max(2, 2 * flag_total // owner_total)
    onehot = (owner[:, None] == jnp.arange(owner_total, dtype=jnp.int32)[None, :]).astype(jnp.int32)
    before = jnp.cumsum(onehot, axis=0) - onehot
    slot_index = jnp.sum(before * onehot, axis=1)
    target = jnp.where(live_rows, owner * capacity + slot_index, owner_total * capacity)
    outgoing = jnp.zeros((owner_total * capacity, environ.shape[1], env_width), jnp.bfloat16)
    outgoing = outgoing.at[target].set(environ, mode="drop")
    slot_live = (
        jnp.zeros((owner_total * capacity,), jnp.bfloat16)
        .at[target]
        .set(jnp.ones((flag_total,), jnp.bfloat16), mode="drop")
    )
    local_first = w_first[0]
    local_head = w_head[0]
    results = specialist(
        lax.all_to_all(
            outgoing.reshape(owner_total, capacity, environ.shape[1], env_width),
            ("gx", "gy"),
            split_axis=0,
            concat_axis=0,
            tiled=True,
        ),
        lax.all_to_all(
            slot_live.reshape(owner_total, capacity),
            ("gx", "gy"),
            split_axis=0,
            concat_axis=0,
            tiled=True,
        ),
        local_first,
        local_head,
    )
    returned = lax.all_to_all(results, ("gx", "gy"), split_axis=0, concat_axis=0, tiled=True)
    returned = returned.reshape(owner_total * capacity, 3)
    correction = returned[jnp.minimum(target, owner_total * capacity - 1)] * live_rows[
        :, None
    ].astype(jnp.float32)
    forces = base_force.at[:, local_ids].add(correction.T)
    return forces.reshape(3, cells_x, cells_y, depth)


def solution(mesh):
    placed = (
        P("gx", "gy", "gz", None),
        P("gx", "gy", "gz", None),
        P("gx", "gy", "gz", None),
        P(),
        P(),
        P(),
        P(),
        P(),
        P(("gx", "gy"), None, None),
        P(("gx", "gy"), None, None),
        P("gx", "gy", "gz", None),
        P("gx", "gy", "gz", None, None),
        P("gx", "gy", "gz"),
    )
    return jax.shard_map(
        per_device, mesh=mesh, in_specs=placed, out_specs=P(None, "gx", "gy", "gz"), check_vma=False
    )
```

profile of v0, /device:TPU:0, one launch (start us, length us, event | category | flops | bytes accessed | tf_op | source)
XLA Modules:
  0.0 185.0 jit_solution(1224427024891552187)
XLA Ops:
  0.0 0.8 fusion.82
  0.8 4.9 %collective-permute-start = (bf16[1,4,4,256]{3,2,1,0:T(4,128)(2,1)S(1)}, bf16[1,4,4,256]{3,2,1,0:T(4,128)(2,1)S(1)}, u32[]{:S(2)}, u32[]{:S(2)}) collective-permute-start(bf16[1,4,4,256]{3,2,1,0:T(4,128)(2,1)S(1)} %get-tuple-element.107), channel_id=1, source_target_pairs={{0,1},{1,2},{2,3},{4,5},{5,6},{6,7},{8,9},{9,10},{10,11},{12,13},{... | collective-permute-start | bytes 24584 | tf_op jit(solution)/shard_map/ppermute | solution.py:25
  5.7 1.3 collective-permute-start.1
  7.0 1.1 compare_select_fusion
  8.2 1.1 add_multiply_fusion
  9.3 0.8 fusion.84
  10.0 0.7 fusion.63
  10.8 0.8 select_reduce_fusion
  12.3 0.9 pad_maximum_fusion.3
  13.2 1.6 collective-permute-start.2
  14.8 0.5 collective-permute-start.3
  15.3 0.7 fusion.72
  16.0 2.5 %collective-permute-done.2 = bf16[1,4,40,256]{3,2,1,0:T(8,128)(2,1)S(1)} collective-permute-done((bf16[1,4,40,256]{3,2,1,0:T(8,128)(2,1)S(1)}, bf16[1,4,40,256]{3,2,1,0:T(8,128)(2,1)S(1)}, u32[]{:S(2)}, u32[]{:S(2)}) %collective-permute-start.2) | collective-permute-done | bytes 81952 | tf_op jit(solution)/shard_map/ppermute | solution.py:25
  18.4 0.9 collective-permute-done.3
  19.3 0.8 pad_maximum_fusion.14
  20.1 1.7 collective-permute-start.5
  21.8 1.9 %collective-permute-done.4 = bf16[3,1,40,256]{3,2,1,0:T(8,128)(2,1)S(1)} collective-permute-done((bf16[3,1,40,256]{3,2,1,0:T(8,128)(2,1)S(1)}, bf16[3,1,40,256]{3,2,1,0:T(8,128)(2,1)S(1)}, u32[]{:S(2)}, u32[]{:S(2)}) %collective-permute-start.4) | collective-permute-done | bytes 61472 | tf_op jit(solution)/shard_map/ppermute | solution.py:25
  23.7 0.9 pad_maximum_fusion
  24.6 33.1 %gather_fusion = bf16[8192,256]{1,0:T(8,128)(2,1)} fusion(bf16[720,256]{1,0:T(8,128)(2,1)S(1)} %bitcast.134, s32[8192]{0:T(1024)S(1)} %broadcast_clamp_fusion), kind=kCustom, calls=%fused_computation | custom fusion | bytes 8421376 | tf_op jit(solution)/shard_map/while/body/eval_jaxpr/gather | solution.py:76
  57.8 3.1 %convolution_convert_fusion.1 = bf16[128,8,256]{2,1,0:T(8,128)(2,1)S(1)} fusion(bf16[128,64,256]{2,1,0:T(8,128)(2,1)} %bitcast.137, f32[128,64]{1,0:T(8,128)S(1)} %add_multiply_fusion, f32[8]{0:T(128)S(1)} %multiply_add_fusion, f32[128,64]{1,0:T(8,128)S(1)} %bitcast.151), kind=kOutput, calls=%fused_computation.21 | convolution fusion | flops 34144256 | bytes 4784160 | tf_op jit(solution)/shard_map/while/body/eval_jaxpr/ask,asf->akf/dot_general | solution.py:77
  61.0 0.6 multiply_reduce_fusion.1
  61.7 4.5 %collective-permute-start.6 = (bf16[1,4,4,256]{3,2,1,0:T(4,128)(2,1)S(1)}, bf16[1,4,4,256]{3,2,1,0:T(4,128)(2,1)S(1)}, u32[]{:S(2)}, u32[]{:S(2)}) collective-permute-start(bf16[1,4,4,256]{3,2,1,0:T(4,128)(2,1)S(1)} %get-tuple-element.105), channel_id=1, source_target_pairs={{0,1},{1,2},{2,3},{4,5},{5,6},{6,7},{8,9},{9,10},{10,11},{12,13},{... | collective-permute-start | bytes 24584 | tf_op jit(solution)/shard_map/ppermute | solution.py:25
  66.2 1.3 collective-permute-start.7
  67.5 0.8 scatter_custom_fusion
  68.3 0.7 all_to_all.16
  68.9 3.3 %all-to-all-start = ((bf16[8,1,8]{2,1,0:T(2,128)(2,1)}), bf16[8,1,8]{2,1,0:T(2,128)(2,1)S(1)}, u32[]{:S(2)}, u32[]{:S(2)}) async-start(bf16[8,1,8]{2,1,0:T(2,128)(2,1)} %all_to_all.16), calls=%async_computation | async-start | bytes 8192 | tf_op jit(solution)/shard_map/all_to_all | solution.py:191
  72.3 2.0 %collective-permute-start.8 = (bf16[1,4,40,256]{3,2,1,0:T(8,128)(2,1)S(1)}, bf16[1,4,40,256]{3,2,1,0:T(8,128)(2,1)S(1)}, u32[]{:S(2)}, u32[]{:S(2)}) collective-permute-start(bf16[1,4,40,256]{3,2,1,0:T(8,128)(2,1)S(1)} %pad_maximum_fusion.4), channel_id=1, source_target_pairs={{0,16},{16,0},{1,17},{17,1},{2,18},{18,2},{3,19},{19,3},{4,20},{20... | collective-permute-start | bytes 245768 | tf_op jit(solution)/shard_map/ppermute | solution.py:25
  74.4 0.2 fusion.44
  74.6 2.8 %collective-permute-done.8 = bf16[1,4,40,256]{3,2,1,0:T(8,128)(2,1)S(1)} collective-permute-done((bf16[1,4,40,256]{3,2,1,0:T(8,128)(2,1)S(1)}, bf16[1,4,40,256]{3,2,1,0:T(8,128)(2,1)S(1)}, u32[]{:S(2)}, u32[]{:S(2)}) %collective-permute-start.8) | collective-permute-done | bytes 81952 | tf_op jit(solution)/shard_map/ppermute | solution.py:25
  77.4 2.1 %collective-permute-done.9 = bf16[1,4,40,256]{3,2,1,0:T(8,128)(2,1)S(1)} collective-permute-done((bf16[1,4,40,256]{3,2,1,0:T(8,128)(2,1)S(1)}, bf16[1,4,40,256]{3,2,1,0:T(8,128)(2,1)S(1)}, u32[]{:S(2)}, u32[]{:S(2)}) %collective-permute-start.9) | collective-permute-done | bytes 81952 | tf_op jit(solution)/shard_map/ppermute | solution.py:27
  79.6 1.7 collective-permute-start.11
  81.3 1.9 %collective-permute-done.10 = bf16[3,1,40,256]{3,2,1,0:T(8,128)(2,1)S(1)} collective-permute-done((bf16[3,1,40,256]{3,2,1,0:T(8,128)(2,1)S(1)}, bf16[3,1,40,256]{3,2,1,0:T(8,128)(2,1)S(1)}, u32[]{:S(2)}, u32[]{:S(2)}) %collective-permute-start.10) | collective-permute-done | bytes 61472 | tf_op jit(solution)/shard_map/ppermute | solution.py:25
  83.2 33.1 %gather_fusion.1 = bf16[8192,256]{1,0:T(8,128)(2,1)} fusion(bf16[720,256]{1,0:T(8,128)(2,1)S(1)} %bitcast.133, s32[8192]{0:T(1024)S(1)} %broadcast_clamp_fusion), kind=kCustom, calls=%fused_computation.1 | custom fusion | bytes 8421376 | tf_op jit(solution)/shard_map/while/body/eval_jaxpr/gather | solution.py:76
  116.3 2.9 %convolution_convert_fusion = bf16[128,8,256]{2,1,0:T(8,128)(2,1)S(1)} fusion(bf16[128,64,256]{2,1,0:T(8,128)(2,1)} %bitcast.136, f32[128,64]{1,0:T(8,128)S(1)} %add_multiply_fusion, f32[8]{0:T(128)S(1)} %multiply_add_fusion, f32[128,64]{1,0:T(8,128)S(1)} %bitcast.152), kind=kOutput, calls=%fused_computation.20 | convolution fusion | flops 34144256 | bytes 4784160 | tf_op jit(solution)/shard_map/while/body/eval_jaxpr/ask,asf->akf/dot_general | solution.py:77
  119.4 0.6 multiply_reduce_fusion
  119.9 0.2 convolution_convert_fusion.2
  120.2 4.5 %collective-permute-start.12 = (bf16[1,4,4,128]{3,2,1,0:T(4,128)(2,1)S(1)}, bf16[1,4,4,128]{3,2,1,0:T(4,128)(2,1)S(1)}, u32[]{:S(2)}, u32[]{:S(2)}) collective-permute-start(bf16[1,4,4,128]{3,2,1,0:T(4,128)(2,1)S(1)} %get-tuple-element.109), channel_id=1, source_target_pairs={{0,1},{1,2},{2,3},{4,5},{5,6},{6,7},{8,9},{9,10},{10,11},{12,13},{... | collective-permute-start | bytes 12296 | tf_op jit(solution)/shard_map/ppermute | solution.py:25
  124.7 1.3 collective-permute-start.13
  126.0 0.6 gather_fusion.3
  126.6 3.6 %collective-permute-done.13 = bf16[1,4,4,128]{3,2,1,0:T(4,128)(2,1)S(1)} collective-permute-done((bf16[1,4,4,128]{3,2,1,0:T(4,128)(2,1)S(1)}, bf16[1,4,4,128]{3,2,1,0:T(4,128)(2,1)S(1)}, u32[]{:S(2)}, u32[]{:S(2)}) %collective-permute-start.13) | collective-permute-done | bytes 4128 | tf_op jit(solution)/shard_map/ppermute | solution.py:27
  130.2 1.2 collective-permute-start.14
  131.4 0.9 collective-permute-start.15
  132.4 2.3 %collective-permute-done.14 = bf16[1,4,40,128]{3,2,1,0:T(8,128)(2,1)S(1)} collective-permute-done((bf16[1,4,40,128]{3,2,1,0:T(8,128)(2,1)S(1)}, bf16[1,4,40,128]{3,2,1,0:T(8,128)(2,1)S(1)}, u32[]{:S(2)}, u32[]{:S(2)}) %collective-permute-start.14) | collective-permute-done | bytes 40992 | tf_op jit(solution)/shard_map/ppermute | solution.py:25
  134.7 0.7 collective-permute-done.15
  135.5 1.7 collective-permute-start.17
  137.2 0.6 gather_fusion.2
  137.8 1.0 collective-permute-done.16
  138.8 6.2 %gather_fusion.4 = bf16[2048,128]{1,0:T(8,128)(2,1)S(1)} fusion(bf16[720,128]{1,0:T(8,128)(2,1)S(1)} %bitcast.135, s32[2048]{0:T(1024)S(1)} %broadcast_clamp_fusion.1), kind=kCustom, calls=%fused_computation.4 | custom fusion | bytes 1056768 | tf_op jit(solution)/shard_map/gather | solution.py:166
  145.1 0.3 fusion.6
  145.4 1.2 broadcast_in_dim.61
  146.6 4.3 %scatter_fusion = bf16[64,64,128]{2,1,0:T(8,128)(2,1)} fusion(bf16[64,64,128]{2,1,0:T(8,128)(2,1)} %broadcast_in_dim.61, s32[32]{0:T(128)S(1)} %fusion.71, bf16[32,64,128]{2,1,0:T(8,128)(2,1)S(1)} %fusion.6), kind=kCustom, calls=%fused_computation.8 | custom fusion | bytes 1572992 | tf_op jit(solution)/shard_map/scatter | solution.py:175
  150.9 3.6 %all-to-all-start.1 = ((bf16[8,8,64,128]{3,2,1,0:T(8,128)(2,1)}), bf16[8,8,64,128]{3,2,1,0:T(8,128)(2,1)S(1)}, u32[]{:S(2)}, u32[]{:S(2)}) async-start(bf16[8,8,64,128]{3,2,1,0:T(8,128)(2,1)} %bitcast.28), calls=%async_computation.1 | async-start | bytes 2097152 | tf_op jit(solution)/shard_map/all_to_all | solution.py:184
  154.5 0.6 convert_reduce_fusion.2
  156.0 2.0 %sort.17 = (s32[64]{0:T(128)}, s32[64]{0:T(128)S(1)}) sort(s32[64]{0:T(128)S(1)} %select_n.240, s32[64]{0:T(128)S(1)} %iota.50), dimensions={0}, to_apply=%region_5.6 | sort | flops 384 | bytes 1024 | tf_op jit(solution)/shard_map/jit(argsort)/sort | solution.py:103
  158.1 11.8 %all-to-all-done.1 = bf16[8,8,64,128]{3,2,1,0:T(8,128)(2,1)S(1)} async-done(((bf16[8,8,64,128]{3,2,1,0:T(8,128)(2,1)}), bf16[8,8,64,128]{3,2,1,0:T(8,128)(2,1)S(1)}, u32[]{:S(2)}, u32[]{:S(2)}) %all-to-all-start.1) | async-done | bytes 1048608 | tf_op jit(solution)/shard_map/all_to_all | solution.py:184
  169.8 0.7 gather_fusion.5
  170.6 1.6 while.2
  170.6 1.3 convert_reduce_fusion.4
  172.3 0.8 scatter_custom_fusion.2
  173.1 0.7 copy.24
  173.8 4.7 %all-to-all-start.2 = ((f32[8,8,3]{1,2,0:T(4,128)}), f32[8,8,3]{1,2,0:T(4,128)S(1)}, u32[]{:S(2)}, u32[]{:S(2)}) async-start(f32[8,8,3]{1,2,0:T(4,128)} %copy.24), calls=%async_computation.2 | async-start | bytes 32768 | tf_op jit(solution)/shard_map/all_to_all | solution.py:201
  178.9 4.4 %all-to-all-done.2 = f32[8,8,3]{1,2,0:T(4,128)S(1)} async-done(((f32[8,8,3]{1,2,0:T(4,128)}), f32[8,8,3]{1,2,0:T(4,128)S(1)}, u32[]{:S(2)}, u32[]{:S(2)}) %all-to-all-start.2) | async-done | bytes 800 | tf_op jit(solution)/shard_map/all_to_all | solution.py:201
  183.4 0.8 scatter_custom_fusion.3
  184.3 0.7 copy.27
  (75 shorter events, 2.1 us)
Async XLA Ops:
  0.0 119.9 %copy-start = (bf16[256,128]{1,0:T(8,128)(2,1)S(1)}, bf16[256,128]{1,0:T(8,128)(2,1)}, u32[]{:S(2)}) copy-start(bf16[256,128]{1,0:T(8,128)(2,1)} %param.21) | copy-start | bytes 196612
  0.8 11.5 %collective-permute-start = (bf16[1,4,4,256]{3,2,1,0:T(4,128)(2,1)S(1)}, bf16[1,4,4,256]{3,2,1,0:T(4,128)(2,1)S(1)}, u32[]{:S(2)}, u32[]{:S(2)}) collective-permute-start(bf16[1,4,4,256]{3,2,1,0:T(4,128)(2,1)S(1)} %get-tuple-element.107), channel_id=1, source_target_pairs={{0,1},{1,2},{2,3},{4,5},{5,6},{6,7},{8,9},{9,10},{10,11},{12,13},{... | collective-permute-start | bytes 24584 | tf_op jit(solution)/shard_map/ppermute | solution.py:25
  5.7 6.6 %collective-permute-start.1 = (bf16[1,4,4,256]{3,2,1,0:T(4,128)(2,1)S(1)}, bf16[1,4,4,256]{3,2,1,0:T(4,128)(2,1)S(1)}, u32[]{:S(2)}, u32[]{:S(2)}) collective-permute-start(bf16[1,4,4,256]{3,2,1,0:T(4,128)(2,1)S(1)} %get-tuple-element.108), channel_id=1, source_target_pairs={{1,0},{2,1},{3,2},{5,4},{6,5},{7,6},{9,8},{10,9},{11,10},{13,12},{... | collective-permute-start | bytes 24584 | tf_op jit(solution)/shard_map/ppermute | solution.py:27
  13.2 5.2 %collective-permute-start.2 = (bf16[1,4,40,256]{3,2,1,0:T(8,128)(2,1)S(1)}, bf16[1,4,40,256]{3,2,1,0:T(8,128)(2,1)S(1)}, u32[]{:S(2)}, u32[]{:S(2)}) collective-permute-start(bf16[1,4,40,256]{3,2,1,0:T(8,128)(2,1)S(1)} %pad_maximum_fusion.3), channel_id=1, source_target_pairs={{0,16},{16,0},{1,17},{17,1},{2,18},{18,2},{3,19},{19,3},{4,20},{20... | collective-permute-start | bytes 245768 | tf_op jit(solution)/shard_map/ppermute | solution.py:25
  14.8 4.5 %collective-permute-start.3 = (bf16[1,4,40,256]{3,2,1,0:T(8,128)(2,1)S(1)}, bf16[1,4,40,256]{3,2,1,0:T(8,128)(2,1)S(1)}, u32[]{:S(2)}, u32[]{:S(2)}) collective-permute-start(bf16[1,4,40,256]{3,2,1,0:T(8,128)(2,1)S(1)} %pad_maximum_fusion.3), channel_id=1, source_target_pairs={{16,0},{0,16},{17,1},{1,17},{18,2},{2,18},{19,3},{3,19},{20,4},{4,... | collective-permute-start | bytes 245768 | tf_op jit(solution)/shard_map/ppermute | solution.py:27
  20.0 3.7 %collective-permute-start.4 = (bf16[3,1,40,256]{3,2,1,0:T(8,128)(2,1)S(1)}, bf16[3,1,40,256]{3,2,1,0:T(8,128)(2,1)S(1)}, u32[]{:S(2)}, u32[]{:S(2)}) collective-permute-start(bf16[3,1,40,256]{3,2,1,0:T(8,128)(2,1)S(1)} %get-tuple-element.101), channel_id=1, source_target_pairs={{0,4},{4,8},{8,12},{12,0},{1,5},{5,9},{9,13},{13,1},{2,6},{6,10},{... | collective-permute-start | bytes 184328 | tf_op jit(solution)/shard_map/ppermute | solution.py:25
  20.1 3.6 %collective-permute-start.5 = (bf16[3,1,40,256]{3,2,1,0:T(8,128)(2,1)S(1)}, bf16[3,1,40,256]{3,2,1,0:T(8,128)(2,1)S(1)}, u32[]{:S(2)}, u32[]{:S(2)}) collective-permute-start(bf16[3,1,40,256]{3,2,1,0:T(8,128)(2,1)S(1)} %get-tuple-element.102), channel_id=1, source_target_pairs={{4,0},{8,4},{12,8},{0,12},{5,1},{9,5},{13,9},{1,13},{6,2},{10,6},{... | collective-permute-start | bytes 184328 | tf_op jit(solution)/shard_map/ppermute | solution.py:27
  24.6 33.1 %copy-start.2 = (f32[1,4,32,64]{3,2,1,0:T(8,128)S(1)}, f32[1,4,32,64]{3,2,1,0:T(8,128)}, u32[]{:S(2)}) copy-start(f32[1,4,32,64]{3,2,1,0:T(8,128)} %param.17) | copy-start | bytes 98308
  57.7 3.2 %copy-start.1 = (bf16[1,4,32,256]{3,2,1,0:T(8,128)(2,1)S(1)}, bf16[1,4,32,256]{3,2,1,0:T(8,128)(2,1)}, u32[]{:S(2)}) copy-start(bf16[1,4,32,256]{3,2,1,0:T(8,128)(2,1)} %param.15) | copy-start | bytes 196612
  57.7 3.2 %copy-start.6 = (bf16[2,2048,256]{2,1,0:T(8,128)(2,1)S(1)}, bf16[2,2048,256]{2,1,0:T(8,128)(2,1)}, u32[]{:S(2)}) copy-start(bf16[2,2048,256]{2,1,0:T(8,128)(2,1)} %param.18) | copy-start | bytes 6291460
  57.7 3.2 %copy-start.7 = (bf16[2,256,256]{2,1,0:T(8,128)(2,1)S(1)}, bf16[2,256,256]{2,1,0:T(8,128)(2,1)}, u32[]{:S(2)}) copy-start(bf16[2,256,256]{2,1,0:T(8,128)(2,1)} %param.19) | copy-start | bytes 786436
  57.7 16.7 %copy-start.3 = (s32[1,4,32,64]{3,2,1,0:T(8,128)S(1)}, s32[1,4,32,64]{3,2,1,0:T(8,128)}, u32[]{:S(2)}) copy-start(s32[1,4,32,64]{3,2,1,0:T(8,128)} %param.16) | copy-start | bytes 98308
  57.7 23.6 %copy-start.9 = (s32[1,1,1,32]{3,2,1,0:T(1,128)S(1)}, s32[1,1,1,32]{3,2,1,0:T(1,128)}, u32[]{:S(2)}) copy-start(s32[1,1,1,32]{3,2,1,0:T(1,128)} %param.25) | copy-start | bytes 388
  61.7 10.6 %collective-permute-start.6 = (bf16[1,4,4,256]{3,2,1,0:T(4,128)(2,1)S(1)}, bf16[1,4,4,256]{3,2,1,0:T(4,128)(2,1)S(1)}, u32[]{:S(2)}, u32[]{:S(2)}) collective-permute-start(bf16[1,4,4,256]{3,2,1,0:T(4,128)(2,1)S(1)} %get-tuple-element.105), channel_id=1, source_target_pairs={{0,1},{1,2},{2,3},{4,5},{5,6},{6,7},{8,9},{9,10},{10,11},{12,13},{... | collective-permute-start | bytes 24584 | tf_op jit(solution)/shard_map/ppermute | solution.py:25
  66.2 6.1 %collective-permute-start.7 = (bf16[1,4,4,256]{3,2,1,0:T(4,128)(2,1)S(1)}, bf16[1,4,4,256]{3,2,1,0:T(4,128)(2,1)S(1)}, u32[]{:S(2)}, u32[]{:S(2)}) collective-permute-start(bf16[1,4,4,256]{3,2,1,0:T(4,128)(2,1)S(1)} %get-tuple-element.106), channel_id=1, source_target_pairs={{1,0},{2,1},{3,2},{5,4},{6,5},{7,6},{9,8},{10,9},{11,10},{13,12},{... | collective-permute-start | bytes 24584 | tf_op jit(solution)/shard_map/ppermute | solution.py:27
  68.9 82.0 %all-to-all-start = ((bf16[8,1,8]{2,1,0:T(2,128)(2,1)}), bf16[8,1,8]{2,1,0:T(2,128)(2,1)S(1)}, u32[]{:S(2)}, u32[]{:S(2)}) async-start(bf16[8,1,8]{2,1,0:T(2,128)(2,1)} %all_to_all.16), calls=%async_computation | async-start | bytes 8192 | tf_op jit(solution)/shard_map/all_to_all | solution.py:191
  72.3 5.1 %collective-permute-start.8 = (bf16[1,4,40,256]{3,2,1,0:T(8,128)(2,1)S(1)}, bf16[1,4,40,256]{3,2,1,0:T(8,128)(2,1)S(1)}, u32[]{:S(2)}, u32[]{:S(2)}) collective-permute-start(bf16[1,4,40,256]{3,2,1,0:T(8,128)(2,1)S(1)} %pad_maximum_fusion.4), channel_id=1, source_target_pairs={{0,16},{16,0},{1,17},{17,1},{2,18},{18,2},{3,19},{19,3},{4,20},{20... | collective-permute-start | bytes 245768 | tf_op jit(solution)/shard_map/ppermute | solution.py:25
  74.3 5.2 %collective-permute-start.9 = (bf16[1,4,40,256]{3,2,1,0:T(8,128)(2,1)S(1)}, bf16[1,4,40,256]{3,2,1,0:T(8,128)(2,1)S(1)}, u32[]{:S(2)}, u32[]{:S(2)}) collective-permute-start(bf16[1,4,40,256]{3,2,1,0:T(8,128)(2,1)S(1)} %pad_maximum_fusion.4), channel_id=1, source_target_pairs={{16,0},{0,16},{17,1},{1,17},{18,2},{2,18},{19,3},{3,19},{20,4},{4,... | collective-permute-start | bytes 245768 | tf_op jit(solution)/shard_map/ppermute | solution.py:27
  79.5 3.7 %collective-permute-start.10 = (bf16[3,1,40,256]{3,2,1,0:T(8,128)(2,1)S(1)}, bf16[3,1,40,256]{3,2,1,0:T(8,128)(2,1)S(1)}, u32[]{:S(2)}, u32[]{:S(2)}) collective-permute-start(bf16[3,1,40,256]{3,2,1,0:T(8,128)(2,1)S(1)} %get-tuple-element.99), channel_id=1, source_target_pairs={{0,4},{4,8},{8,12},{12,0},{1,5},{5,9},{9,13},{13,1},{2,6},{6,10},{... | collective-permute-start | bytes 184328 | tf_op jit(solution)/shard_map/ppermute | solution.py:25
  79.6 3.6 %collective-permute-start.11 = (bf16[3,1,40,256]{3,2,1,0:T(8,128)(2,1)S(1)}, bf16[3,1,40,256]{3,2,1,0:T(8,128)(2,1)S(1)}, u32[]{:S(2)}, u32[]{:S(2)}) collective-permute-start(bf16[3,1,40,256]{3,2,1,0:T(8,128)(2,1)S(1)} %get-tuple-element.100), channel_id=1, source_target_pairs={{4,0},{8,4},{12,8},{0,12},{5,1},{9,5},{13,9},{1,13},{6,2},{10,6},{... | collective-permute-start | bytes 184328 | tf_op jit(solution)/shard_map/ppermute | solution.py:27
  120.2 6.4 %collective-permute-start.12 = (bf16[1,4,4,128]{3,2,1,0:T(4,128)(2,1)S(1)}, bf16[1,4,4,128]{3,2,1,0:T(4,128)(2,1)S(1)}, u32[]{:S(2)}, u32[]{:S(2)}) collective-permute-start(bf16[1,4,4,128]{3,2,1,0:T(4,128)(2,1)S(1)} %get-tuple-element.109), channel_id=1, source_target_pairs={{0,1},{1,2},{2,3},{4,5},{5,6},{6,7},{8,9},{9,10},{10,11},{12,13},{... | collective-permute-start | bytes 12296 | tf_op jit(solution)/shard_map/ppermute | solution.py:25
  124.7 5.5 %collective-permute-start.13 = (bf16[1,4,4,128]{3,2,1,0:T(4,128)(2,1)S(1)}, bf16[1,4,4,128]{3,2,1,0:T(4,128)(2,1)S(1)}, u32[]{:S(2)}, u32[]{:S(2)}) collective-permute-start(bf16[1,4,4,128]{3,2,1,0:T(4,128)(2,1)S(1)} %get-tuple-element.110), channel_id=1, source_target_pairs={{1,0},{2,1},{3,2},{5,4},{6,5},{7,6},{9,8},{10,9},{11,10},{13,12},{... | collective-permute-start | bytes 12296 | tf_op jit(solution)/shard_map/ppermute | solution.py:27
  130.2 4.5 %collective-permute-start.14 = (bf16[1,4,40,128]{3,2,1,0:T(8,128)(2,1)S(1)}, bf16[1,4,40,128]{3,2,1,0:T(8,128)(2,1)S(1)}, u32[]{:S(2)}, u32[]{:S(2)}) collective-permute-start(bf16[1,4,40,128]{3,2,1,0:T(8,128)(2,1)S(1)} %pad_maximum_fusion.15), channel_id=1, source_target_pairs={{0,16},{16,0},{1,17},{17,1},{2,18},{18,2},{3,19},{19,3},{4,20},{20... | collective-permute-start | bytes 122888 | tf_op jit(solution)/shard_map/ppermute | solution.py:25
  131.4 4.0 %collective-permute-start.15 = (bf16[1,4,40,128]{3,2,1,0:T(8,128)(2,1)S(1)}, bf16[1,4,40,128]{3,2,1,0:T(8,128)(2,1)S(1)}, u32[]{:S(2)}, u32[]{:S(2)}) collective-permute-start(bf16[1,4,40,128]{3,2,1,0:T(8,128)(2,1)S(1)} %pad_maximum_fusion.15), channel_id=1, source_target_pairs={{16,0},{0,16},{17,1},{1,17},{18,2},{2,18},{19,3},{3,19},{20,4},{4,... | collective-permute-start | bytes 122888 | tf_op jit(solution)/shard_map/ppermute | solution.py:27
  135.4 3.4 %collective-permute-start.16 = (bf16[3,1,40,128]{3,2,1,0:T(8,128)(2,1)S(1)}, bf16[3,1,40,128]{3,2,1,0:T(8,128)(2,1)S(1)}, u32[]{:S(2)}, u32[]{:S(2)}) collective-permute-start(bf16[3,1,40,128]{3,2,1,0:T(8,128)(2,1)S(1)} %get-tuple-element.103), channel_id=1, source_target_pairs={{0,4},{4,8},{8,12},{12,0},{1,5},{5,9},{9,13},{13,1},{2,6},{6,10},{... | collective-permute-start | bytes 92168 | tf_op jit(solution)/shard_map/ppermute | solution.py:25
  135.5 3.3 %collective-permute-start.17 = (bf16[3,1,40,128]{3,2,1,0:T(8,128)(2,1)S(1)}, bf16[3,1,40,128]{3,2,1,0:T(8,128)(2,1)S(1)}, u32[]{:S(2)}, u32[]{:S(2)}) collective-permute-start(bf16[3,1,40,128]{3,2,1,0:T(8,128)(2,1)S(1)} %get-tuple-element.104), channel_id=1, source_target_pairs={{4,0},{8,4},{12,8},{0,12},{5,1},{9,5},{13,9},{1,13},{6,2},{10,6},{... | collective-permute-start | bytes 92168 | tf_op jit(solution)/shard_map/ppermute | solution.py:27
  145.0 25.6 %copy-start.4 = (bf16[1,3,1024]{2,1,0:T(4,128)(2,1)S(1)}, bf16[1,3,1024]{2,1,0:T(4,128)(2,1)}, u32[]{:S(2)}) copy-start(bf16[1,3,1024]{2,1,0:T(4,128)(2,1)} %param.24) | copy-start | bytes 18436
  145.0 25.6 %copy-start.8 = (bf16[1,128,1024]{2,1,0:T(8,128)(2,1)S(1)}, bf16[1,128,1024]{2,1,0:T(8,128)(2,1)}, u32[]{:S(2)}) copy-start(bf16[1,128,1024]{2,1,0:T(8,128)(2,1)} %param.23) | copy-start | bytes 786436
  150.9 18.9 %all-to-all-start.1 = ((bf16[8,8,64,128]{3,2,1,0:T(8,128)(2,1)}), bf16[8,8,64,128]{3,2,1,0:T(8,128)(2,1)S(1)}, u32[]{:S(2)}, u32[]{:S(2)}) async-start(bf16[8,8,64,128]{3,2,1,0:T(8,128)(2,1)} %bitcast.28), calls=%async_computation.1 | async-start | bytes 2097152 | tf_op jit(solution)/shard_map/all_to_all | solution.py:184
  170.6 7.9 %copy-start.5 = (bf16[3,256]{1,0:T(4,128)(2,1)S(1)}, bf16[3,256]{1,0:T(4,128)(2,1)}, u32[]{:S(2)}) copy-start(bf16[3,256]{1,0:T(4,128)(2,1)} %param.22) | copy-start | bytes 4612
  173.8 9.5 %all-to-all-start.2 = ((f32[8,8,3]{1,2,0:T(4,128)}), f32[8,8,3]{1,2,0:T(4,128)S(1)}, u32[]{:S(2)}, u32[]{:S(2)}) async-start(f32[8,8,3]{1,2,0:T(4,128)} %copy.24), calls=%async_computation.2 | async-start | bytes 32768 | tf_op jit(solution)/shard_map/all_to_all | solution.py:201
where the time goes:
time: 186 us; the launch traced here: 185 us
  local copies, waits for them, and re-layouts  85.9 us (46%)
  starting transfers between devices  41 us (22%)
  waiting for transfers between devices  35.8 us (19%)
  other arithmetic  11.4 us (6%)
  matrix products  8.92 us (5%)
    gather x2, local copies, waits for them, and re-layouts, one_block(): nearby = flat_rows[row_index]  66.2 us
    ppermute x9, starting transfers between devices, with_halo(): lax.ppermute(tail, axis, [(i, (i + 1) % count) for i in range(ends)])  18.9 us
    ppermute x9, waiting for transfers between devices, with_halo(): lax.ppermute(tail, axis, [(i, (i + 1) % count) for i in range(ends)])  12.4 us
    all_to_all x1, waiting for transfers between devices, per_device(): lax.all_to_all(outgoing.reshape(owner_total, capacity, environ.shape[1],...  11.8 us
    ppermute x9, starting transfers between devices, with_halo(): lax.ppermute(head, axis, [((i + 1) % count, i) for i in range(ends)])  10.6 us
    ppermute x9, waiting for transfers between devices, with_halo(): lax.ppermute(head, axis, [((i + 1) % count, i) for i in range(ends)])  7.22 us
    gather x2, local copies, waits for them, and re-layouts, per_device(): nearby = proj_rows[row_index[local_ids]]  6.75 us
    dot_general x2, matrix products, one_block(): jnp.einsum('ask,asf->akf', radial_basis, nearby, preferred_element_type=j...  5.95 us
  transfers between devices with their start and end apart: 21, of which 12 were waited for; matrix products, arithmetic and copies ran while one was open for 32% of the time, Pallas kernels for 0%

commit v1 on v0

v1 whole, which is shorter than its diff:
```python
import functools

import jax
import jax.numpy as jnp
from jax import lax
from jax.experimental import pallas as pl
from jax.experimental.pallas import tpu as pltpu
from jax.sharding import PartitionSpec as P

M = 4
NRB = 8
L = 2
ROWS = 256
F32 = jnp.float32
BF16 = jnp.bfloat16
MESH = pl.DeviceIdType.MESH


def iota(shape, dim):
    return lax.broadcasted_iota(jnp.int32, shape, dim)


def plane_buffers(n_gx):
    return (1, 0, 1) if n_gx == 2 else (1, 0, 2)


def messages(n_gx):
    steps_x = (0, 1) if n_gx == 2 else (0, 1, -1)
    return [
        (dx, dy, dz)
        for dx in steps_x
        for dy in (0, 1, -1)
        for dz in (0, 1, -1)
        if (dx, dy, dz) != (0, 0, 0)
    ]


def cutoff_of(distance):
    half = distance * (jnp.pi / 10.0)
    sq = half * half
    term = -1.0 / 87178291200.0
    for coef in (1 / 479001600.0, -1 / 3628800.0, 1 / 40320.0, -1 / 720.0, 1 / 24.0, -0.5, 1.0):
        term = term * sq + coef
    return term * term


def face_selector():
    row = iota((96, 128), 0)
    atom = iota((96, 128), 1)
    part = row >> 4
    y = (row & 15) >> 2
    j = row & 3
    g = part - 2
    corner_y = jnp.where((g & 1) == 0, 3, 0)
    corner_z = jnp.where(g < 2, 28, 0)
    corner = jnp.where(y == g, corner_y * 32 + corner_z + j, -1)
    target = jnp.where(part == 0, y * 32 + j, jnp.where(part == 1, y * 32 + 28 + j, corner))
    return jnp.where(atom == target, 1.0, 0.0).astype(BF16)


def candidate_offsets():
    row = iota((ROWS, 128), 0)
    atom = iota((ROWS, 128), 1)
    own_y = atom >> 5
    own_z = (atom & 31) >> 2
    tail = row - 192
    group = (row & 15) >> 2
    col_tail = jnp.where(tail < 32, group + 1, jnp.where((group & 1) == 0, 0, 5))
    col_tail = jnp.where(tail < 48, col_tail, -20)
    z_tail = jnp.where(tail < 16, -1, jnp.where(tail < 32, 8, jnp.where(group < 2, -1, 8)))
    col = jnp.where(row < 192, row >> 5, col_tail)
    z = jnp.where(row < 192, (row & 31) >> 2, z_tail)
    oy = col - own_y
    oz = z - own_z + 1
    good = (oy >= 0) & (oy <= 2) & (oz >= 0) & (oz <= 2)
    return jnp.where(good, oy * 3 + oz, -1)


def potential_kernel(
    sizes,
    feat,
    code,
    dist,
    wm_hbm,
    w_update,
    gain,
    w_env,
    w_out,
    planes_out,
    base_out,
    weights,
    slots,
    dcode,
    offsets,
    near,
    near_proj,
    corner,
    corner_proj,
    packs,
    packs_proj,
    state_ref,
    proj_ref,
    wm,
    send_sem,
    recv_sem,
    wm_sem,
):
    n_gx, n_gy, n_gz = sizes
    buffer_of = plane_buffers(n_gx)
    n_buf = max(buffer_of) + 1
    todo = messages(n_gx)
    me = (lax.axis_index("gx"), lax.axis_index("gy"), lax.axis_index("gz"))

    def target(step):
        return (
            lax.rem(me[0] + step[0] + n_gx, n_gx),
            lax.rem(me[1] + step[1] + n_gy, n_gy),
            me[2] + step[2],
        )

    def along_z(dz, act):
        if dz == 0:
            act()
        elif dz > 0:
            pl.when(me[2] < n_gz - 1)(act)
        else:
            pl.when(me[2] > 0)(act)

    for b in range(n_buf):
        for e in range(2):
            near[e, b, 192:256, :] = jnp.zeros((64, near.shape[-1]), BF16)
        near_proj[b, 192:256, :] = jnp.zeros((64, near_proj.shape[-1]), BF16)
    corner[...] = jnp.zeros(corner.shape, BF16)
    corner_proj[...] = jnp.zeros(corner_proj.shape, BF16)

    barrier = pltpu.get_barrier_semaphore()
    for step in todo:

        def greet(step=step):
            pl.semaphore_signal(barrier, inc=1, device_id=target(step), device_id_type=MESH)

        along_z(step[2], greet)

    weight_copy = pltpu.make_async_copy(wm_hbm, wm, wm_sem)
    weight_copy.start()

    selector = face_selector()

    def copies(e, source, packed, plane, corners):
        made = []
        for index, (dx, dy, dz) in enumerate(todo):
            b = 0 if dx == 0 else buffer_of[0 if dx > 0 else 2]
            if dz == 0:
                if dy == 0:
                    src, dst = source, plane.at[b, pl.ds(32, 128)]
                elif dy > 0:
                    src, dst = source.at[pl.ds(96, 32)], plane.at[b, pl.ds(0, 32)]
                else:
                    src, dst = source.at[pl.ds(0, 32)], plane.at[b, pl.ds(160, 32)]
            elif dy == 0:
                src = packed.at[pl.ds(16 if dz > 0 else 0, 16)]
                dst = plane.at[b, pl.ds(192 if dz > 0 else 208, 16)]
            else:
                g = (0 if dz > 0 else 2) + (0 if dy > 0 else 1)
                src, dst = packed.at[pl.ds(32 + 16 * g, 16)], corners.at[b, g]
            made.append(
                pltpu.make_async_remote_copy(
                    src_ref=src,
                    dst_ref=dst,
                    send_sem=send_sem.at[e, index],
                    recv_sem=recv_sem.at[e, index],
                    device_id=target((dx, dy, dz)),
                    device_id_type=MESH,
                )
            )
        return made

    def send_all(made):
        for step, copy in zip(todo, made):
            along_z(step[2], copy.start)

    def receive_all(made, plane, corners):
        for step, copy in zip(todo, made):
            along_z(-step[2], copy.wait_recv)
        for b in range(n_buf):
            tile = corners[b, 0].astype(F32)
            for g in range(1, 4):
                tile = tile + corners[b, g].astype(F32)
            plane[b, 224:240, :] = tile.astype(BF16)

    def sent_all(made):
        for step, copy in zip(todo, made):
            along_z(step[2], copy.wait_send)

    def pack(state):
        return jnp.dot(selector, state, preferred_element_type=F32).astype(BF16)

    state = feat[0].reshape(128, feat.shape[-1])
    state_ref[0] = state
    packs[0] = pack(state)
    near[0, 0, 32:160, :] = state

    both = (n_buf) * 3
    here = both - 1
    up = jnp.where(me[2] < n_gz - 1, both, 0)
    down = jnp.where(me[2] > 0, both, 0)
    pl.semaphore_wait(barrier, here + up + down)

    first = copies(0, state_ref.at[0], packs.at[0], near.at[0], corner.at[0])
    send_all(first)

    slot_count = code.shape[-1]
    both_rows = jnp.concatenate(
        [dist[0].reshape(128, slot_count), code[0].reshape(128, slot_count).astype(F32)], axis=1
    )
    slots[...] = both_rows.T
    offsets[...] = candidate_offsets()
    for ox in range(3):
        row = iota((72, 128), 0)
        wanted = (((row >> 3) + 9 * ox) * 4 + (row & 3)).astype(F32)

        def put(s, held):
            named = slots[pl.ds(slot_count + s, 1), :]
            return jnp.where(named == wanted, slots[pl.ds(s, 1), :], held)

        dcode[pl.ds(72 * ox, 72), :] = lax.fori_loop(
            0, slot_count, put, jnp.full((72, 128), -1.0, F32), unroll=8
        )

    for b in range(n_buf):
        for half in range(2):
            where_from = offsets[128 * half : 128 * (half + 1), :]
            parts = []
            for ox in range(3):
                if buffer_of[ox] != b:
                    continue
                dense = jnp.full((128, 128), -1.0, F32)
                for p in range(9):
                    rows = dcode[pl.ds((ox * 9 + p) * 8, 8), :]
                    rows = jnp.broadcast_to(rows[None], (16, 8, 128)).reshape(128, 128)
                    dense = jnp.where(where_from == p, rows, dense)
                dense = dense.T
                parts.append((dense, jnp.where(dense > 0.0, cutoff_of(dense), 0.0)))
            for k in range(NRB):
                total = None
                for dense, cut in parts:
                    gap = dense - (0.8 + k * (4.0 / (NRB - 1)))
                    basis = jnp.exp(-2.0 * (gap * gap)) * cut
                    total = basis if total is None else total + basis
                weights[128 * k : 128 * (k + 1), 256 * b + 128 * half : 256 * b + 128 * (half + 1)] = (
                    total.astype(BF16)
                )

    def layer(l, state):
        width = state.shape[-1]
        rows = near[l].reshape(n_buf * ROWS, width)
        message = jnp.zeros((128, width), F32)
        for k in range(NRB):
            summed = jnp.dot(weights[128 * k : 128 * (k + 1), :], rows, preferred_element_type=F32)
            message = message + jnp.dot(
                summed.astype(BF16),
                wm[l, width * k : width * (k + 1), :],
                preferred_element_type=F32,
            )
        active = (message / (1.0 + jnp.exp(-message))).astype(BF16)
        residual = state.astype(F32) + jnp.dot(active, w_update[l], preferred_element_type=F32)
        inv_rms = lax.rsqrt(jnp.mean(residual * residual, axis=-1, keepdims=True) + 1e-06)
        return (residual * inv_rms * gain[l : l + 1, :]).astype(BF16)

    weight_copy.wait()
    receive_all(first, near.at[0], corner.at[0])
    state = layer(0, state)
    state_ref[1] = state
    packs[1] = pack(state)
    second = copies(1, state_ref.at[1], packs.at[1], near.at[1], corner.at[1])
    send_all(second)
    near[1, 0, 32:160, :] = state
    receive_all(second, near.at[1], corner.at[1])
    state = layer(1, state)
    projected = jnp.dot(state, w_env[...], preferred_element_type=F32).astype(BF16)
    proj_ref[...] = projected
    packs_proj[...] = pack(projected)
    third = copies(2, proj_ref, packs_proj, near_proj, corner_proj)
    send_all(third)
    near_proj[0, 32:160, :] = projected
    base_out[...] = lax.dot_general(
        w_out[...], state, (((1,), (1,)), ((), ())), preferred_element_type=F32
    )
    receive_all(third, near_proj, corner_proj)
    planes_out[...] = near_proj[...].reshape(planes_out.shape)
    sent_all(first)
    sent_all(second)
    sent_all(third)


def specialist_kernel(
    n_gx,
    flag_ids,
    owner,
    flag_count,
    code,
    dist,
    planes,
    base,
    w_first,
    w_head,
    out,
    rows_ref,
    cand_ref,
    picked,
    environ,
):
    buffer_of = plane_buffers(n_gx)
    flags = flag_ids.shape[0]
    slot_count = code.shape[-1]
    codes = code[0].reshape(128, slot_count)
    atom = iota((128, slot_count), 0)
    o = lax.div(codes, M)
    j = codes & 3
    ox = lax.div(o, 9)
    oy = lax.rem(lax.div(o, 3), 3)
    oz = lax.rem(o, 3)
    col = (atom >> 5) + oy
    z = ((atom & 31) >> 2) + oz - 1
    inside = (z >= 0) & (z <= 7)
    top = jnp.where(z > 7, 1, 0)
    side = (col == 0) | (col == 5)
    face = 192 + top * 16 + (col - 1) * 4
    edge = 224 + (top * 2 + jnp.where(col == 5, 1, 0)) * 4
    row = jnp.where(inside, col * 32 + z * 4, jnp.where(side, edge, face)) + j
    plane = jnp.where(ox == 1, 0, jnp.where(ox == 0, buffer_of[0], buffer_of[2]))
    cand_ref[...] = (plane * ROWS + row).astype(F32)
    rows_ref[...] = dist[0].reshape(128, slot_count)
    picked[...] = jnp.zeros((128, 128), F32)

    def pick(r, carry):
        q = flag_ids[r]
        picked[pl.ds(r, 1), 0:slot_count] = rows_ref[pl.ds(q, 1), :]
        picked[pl.ds(r, 1), slot_count : 2 * slot_count] = cand_ref[pl.ds(q, 1), :]
        return carry

    lax.fori_loop(0, flags, pick, 0, unroll=8)
    turned = picked[...].T
    cut = cutoff_of(turned[0:slot_count])
    cand = turned[slot_count : 2 * slot_count]
    lanes = iota((slot_count, planes.shape[0]), 1).astype(F32)
    for r in range(flags):
        chosen = jnp.where(cand[:, r : r + 1] == lanes, 1.0, 0.0).astype(BF16)
        nearby = jnp.dot(chosen, planes[...], preferred_element_type=F32)
        environ[slot_count * r : slot_count * (r + 1), :] = (cut[:, r : r + 1] * nearby).astype(BF16)

    lane = iota(base.shape, 1)

    def correct(r, forces):
        p = owner[r]
        rows = environ[pl.ds(pl.multiple_of(r * slot_count, slot_count), slot_count), :]
        wide = jnp.dot(rows, w_first[p], preferred_element_type=F32)
        hidden = (wide / (1.0 + jnp.exp(-wide))).astype(BF16).astype(F32)
        pooled = (jnp.sum(hidden, axis=0, keepdims=True) * (1.0 / slot_count)).astype(BF16)
        terms = pooled.astype(F32) * w_head[p].astype(F32)
        force = jnp.sum(terms, axis=1, keepdims=True)
        live = jnp.where(r < flag_count[0], 1.0, 0.0)
        return forces + jnp.where(lane == flag_ids[r], force * live, 0.0)

    forces = lax.fori_loop(0, flags, correct, base[...], unroll=4)
    for y in range(out.shape[2]):
        out[:, 0, y, :] = forces[:, 32 * y : 32 * (y + 1)]


def per_device(
    features,
    neighbour_code,
    distance,
    w_message,
    w_update,
    norm_gain,
    w_env,
    w_out,
    w_first,
    w_head,
    flag_ids,
    flag_owner,
    flag_count,
):
    sizes = tuple(lax.axis_size(name) for name in ("gx", "gy", "gz"))
    n_buf = max(plane_buffers(sizes[0])) + 1
    feature_width = features.shape[-1]
    env_width = w_env.shape[-1]
    message_count = len(messages(sizes[0]))
    all_first = lax.all_gather(w_first[0], ("gx", "gy"), axis=0)
    all_head = lax.all_gather(w_head[0], ("gx", "gy"), axis=0)

    vmem = pl.BlockSpec(memory_space=pltpu.VMEM)
    smem = pl.BlockSpec(memory_space=pltpu.SMEM)
    planes, base = pl.pallas_call(
        functools.partial(potential_kernel, sizes),
        out_shape=(
            jax.ShapeDtypeStruct((n_buf * ROWS, env_width), BF16),
            jax.ShapeDtypeStruct((3, 128), F32),
        ),
        in_specs=[vmem, vmem, vmem, pl.BlockSpec(memory_space=pl.ANY)] + [vmem] * 4,
        out_specs=(vmem, vmem),
        scratch_shapes=[
            pltpu.VMEM((NRB * 128, n_buf * ROWS), BF16),
            pltpu.VMEM((128, 128), F32),
            pltpu.VMEM((216, 128), F32),
            pltpu.VMEM((ROWS, 128), jnp.int32),
            pltpu.VMEM((2, n_buf, ROWS, feature_width), BF16),
            pltpu.VMEM((n_buf, ROWS, env_width), BF16),
            pltpu.VMEM((2, n_buf, 4, 16, feature_width), BF16),
            pltpu.VMEM((n_buf, 4, 16, env_width), BF16),
            pltpu.VMEM((2, 96, feature_width), BF16),
            pltpu.VMEM((96, env_width), BF16),
            pltpu.VMEM((2, 128, feature_width), BF16),
            pltpu.VMEM((128, env_width), BF16),
            pltpu.VMEM(w_message.shape, BF16),
            pltpu.SemaphoreType.DMA((3, message_count)),
            pltpu.SemaphoreType.DMA((3, message_count)),
            pltpu.SemaphoreType.DMA,
        ],
        compiler_params=pltpu.CompilerParams(
            collective_id=0, has_side_effects=True, vmem_limit_bytes=32 * 1024 * 1024
        ),
        cost_estimate=pl.CostEstimate(flops=10**9, bytes_accessed=4 * 10**6, transcendentals=10**6),
        name="potential",
    )(features, neighbour_code, distance, w_message, w_update, norm_gain, w_env, w_out)

    owner = flag_owner.reshape(-1)
    if all_first.shape[0] > 8:
        all_first = all_first[owner]
        all_head = all_head[owner]
        owner = jnp.arange(owner.shape[0], dtype=jnp.int32)
    local_ids = flag_ids.reshape(-1)
    flags = local_ids.shape[0]
    slot_count = distance.shape[-1]
    return pl.pallas_call(
        functools.partial(specialist_kernel, sizes[0]),
        out_shape=jax.ShapeDtypeStruct((3,) + features.shape[:3], F32),
        in_specs=[smem] * 3 + [vmem] * 6,
        out_specs=vmem,
        scratch_shapes=[
            pltpu.VMEM((128, slot_count), F32),
            pltpu.VMEM((128, slot_count), F32),
            pltpu.VMEM((128, 128), F32),
            pltpu.VMEM((flags * slot_count, env_width), BF16),
        ],
        compiler_params=pltpu.CompilerParams(vmem_limit_bytes=40 * 1024 * 1024),
        cost_estimate=pl.CostEstimate(
            flops=10**9, bytes_accessed=3 * 10**6, transcendentals=2 * 10**6
        ),
        name="specialist",
    )(
        local_ids,
        owner,
        flag_count.reshape(-1),
        neighbour_code,
        distance,
        planes,
        base,
        all_first,
        all_head,
    )


def solution(mesh):
    placed = (
        P("gx", "gy", "gz", None),
        P("gx", "gy", "gz", None),
        P("gx", "gy", "gz", None),
        P(),
        P(),
        P(),
        P(),
        P(),
        P(("gx", "gy"), None, None),
        P(("gx", "gy"), None, None),
        P("gx", "gy", "gz", None),
        P("gx", "gy", "gz", None, None),
        P("gx", "gy", "gz"),
    )
    return jax.shard_map(
        per_device, mesh=mesh, in_specs=placed, out_specs=P(None, "gx", "gy", "gz"), check_vma=False
    )
```

time: 186 us -> 65.4 us (0.35)
  local copies, waits for them, and re-layouts: 85.9 us -> 8.91 us
  starting transfers between devices: 41 us -> 0.03 us
  waiting for transfers between devices: 35.8 us -> 0.7 us
  Pallas kernels: 0 us -> 30.3 us
  between operations: 1.8 us -> 14.1 us
  other arithmetic: 11.4 us -> 0 us
  blocking collectives: 0 us -> 10.8 us
  matrix products: 8.92 us -> 0 us
    gather x6 -> x0, local copies, waits for them, and re-layouts: 74.2 us -> none  [the longest x2 66.2 us: one_block(): nearby = flat_rows[row_index]]
    pallas_call x0 -> x2, Pallas kernels: none -> 30.3 us  [the longest x1 22.7 us: per_device(): pl.pallas_call(functools.partial(potential_kernel, sizes), out_shape=(jax...]
    ppermute x18 -> x0, starting transfers between devices: 29.5 us -> none  [the longest x9 18.9 us: with_halo(): lax.ppermute(tail, axis, [(i, (i + 1) % count) for i in range(ends)])]
    ppermute x18 -> x0, waiting for transfers between devices: 19.6 us -> none  [the longest x9 12.4 us: with_halo(): lax.ppermute(tail, axis, [(i, (i + 1) % count) for i in range(ends)])]
    all_to_all x3 -> x0, waiting for transfers between devices: 16.2 us -> none  [the longest x1 11.8 us: per_device(): lax.all_to_all(outgoing.reshape(owner_total, capacity, environ.shape[1],...]
    all_to_all x3 -> x0, starting transfers between devices: 11.6 us -> none  [the longest x1 4.7 us: per_device(): lax.all_to_all(results, ('gx', 'gy'), split_axis=0, concat_axis=0, tiled=...]
    all_gather x0 -> x1, blocking collectives: none -> 10.8 us  [per_device(): all_head = lax.all_gather(w_head[0], ('gx', 'gy'), axis=0)]
    dot_general x8 -> x0, matrix products: 8.92 us -> none  [the longest x2 5.95 us: one_block(): jnp.einsum('ask,asf->akf', radial_basis, nearby, preferred_element_type=j...]
  transfers between devices with their start and end apart: 21 -> 1, of which waited for: 12 -> 0; matrix products, arithmetic and copies ran while one was open for 32% -> 0% of each run, Pallas kernels for 0% -> 35%
where the time goes in v1:
time: 65.4 us; the launch traced here: 64.9 us
  Pallas kernels  30.3 us (46%)
  between operations  14.1 us (22%)
  blocking collectives  10.8 us (17%)
  local copies, waits for them, and re-layouts  8.91 us (14%)
  waiting for transfers between devices  0.7 us (1%)
    pallas_call x1, Pallas kernels, per_device(): pl.pallas_call(functools.partial(potential_kernel, sizes), out_shape=(jax...  22.7 us
    all_gather x1, blocking collectives, per_device(): all_head = lax.all_gather(w_head[0], ('gx', 'gy'), axis=0)  10.8 us
    unnamed x26, local copies, waits for them, and re-layouts  8.91 us
    pallas_call x1, Pallas kernels, per_device(): pl.pallas_call(functools.partial(specialist_kernel, sizes[0]), out_shape=...  7.58 us
  transfers between devices with their start and end apart: 1, of which 0 were waited for; matrix products, arithmetic and copies ran while one was open for 0% of the time, Pallas kernels for 35%

profile of v1, /device:TPU:0, one launch (start us, length us, event | category | flops | bytes accessed | tf_op | source)
XLA Modules:
  0.0 64.9 jit_solution(17108615387448729572)
XLA Ops:
  6.5 0.0 copy-start.8
  6.5 0.0 copy-start.6
  6.5 0.0 copy-start.12
  6.5 0.0 copy-start.11
  6.5 0.0 all-gather.2.cloned.1.call-start
  6.6 0.7 %all-gather.2.cloned.1.call-update = ((bf16[1,128,1024]{2,1,0:T(8,128)(2,1)}), bf16[8,128,1024]{2,1,0:T(8,128)(2,1)}) async-update(((), (), s32[]{:S(2)}) %all-gather.2.cloned.1.call-start, bf16[1,128,1024]{2,1,0:T(8,128)(2,1)} %param.21) | async-update | bytes 2621464
  7.9 10.8 %all_gather.7.w_head = bf16[8,3,1024]{2,1,0:T(4,128)(2,1)S(1)} all-gather(bf16[1,3,1024]{2,1,0:T(4,128)(2,1)} %param.22), channel_id=1, replica_groups=mesh['gx'=2,'gy'=4,'gz'=4] {'gx','gy'}, dimensions={0}, use_global_device_ids=true | all-gather | bytes 55296 | tf_op jit(solution)/shard_map/all_gather | solution.py:391
  18.8 0.0 copy-start
  18.8 1.6 %copy-done = bf16[2,2048,256]{2,1,0:T(8,128)(2,1)S(1)} copy-done((bf16[2,2048,256]{2,1,0:T(8,128)(2,1)S(1)}, bf16[2,2048,256]{2,1,0:T(8,128)(2,1)}, u32[]{:S(2)}) %copy-start) | copy-done | bytes 2097176
  20.4 0.0 copy-start.2
  20.4 0.9 %copy-done.2 = bf16[2,256,256]{2,1,0:T(8,128)(2,1)S(1)} copy-done((bf16[2,256,256]{2,1,0:T(8,128)(2,1)S(1)}, bf16[2,256,256]{2,1,0:T(8,128)(2,1)}, u32[]{:S(2)}) %copy-start.2) | copy-done | bytes 262168
  21.3 0.0 copy-start.3
  21.3 0.8 %copy-done.3 = bf16[1,4,32,256]{3,2,1,0:T(8,128)(2,1)S(1)} copy-done((bf16[1,4,32,256]{3,2,1,0:T(8,128)(2,1)S(1)}, bf16[1,4,32,256]{3,2,1,0:T(8,128)(2,1)}, u32[]{:S(2)}) %copy-start.3) | copy-done | bytes 65560
  22.2 0.0 copy-start.4
  22.2 0.8 %copy-done.4 = bf16[256,128]{1,0:T(8,128)(2,1)S(1)} copy-done((bf16[256,128]{1,0:T(8,128)(2,1)S(1)}, bf16[256,128]{1,0:T(8,128)(2,1)}, u32[]{:S(2)}) %copy-start.4) | copy-done | bytes 65560
  23.0 0.0 copy-start.5
  23.0 0.8 %copy-done.5 = s32[1,4,32,64]{3,2,1,0:T(8,128)S(1)} copy-done((s32[1,4,32,64]{3,2,1,0:T(8,128)S(1)}, s32[1,4,32,64]{3,2,1,0:T(8,128)}, u32[]{:S(2)}) %copy-start.5) | copy-done | bytes 32792
  23.9 0.0 copy-start.7
  23.9 0.8 %copy-done.7 = f32[1,4,32,64]{3,2,1,0:T(8,128)S(1)} copy-done((f32[1,4,32,64]{3,2,1,0:T(8,128)S(1)}, f32[1,4,32,64]{3,2,1,0:T(8,128)}, u32[]{:S(2)}) %copy-start.7) | copy-done | bytes 32792
  24.7 0.0 copy-start.9
  24.7 0.7 %copy-done.9 = f32[2,256]{1,0:T(2,128)S(1)} copy-done((f32[2,256]{1,0:T(2,128)S(1)}, f32[2,256]{1,0:T(2,128)}, u32[]{:S(2)}) %copy-start.9) | copy-done | bytes 2072
  25.4 0.0 copy-start.10
  25.4 0.7 %copy-done.10 = bf16[3,256]{1,0:T(4,128)(2,1)S(1)} copy-done((bf16[3,256]{1,0:T(4,128)(2,1)S(1)}, bf16[3,256]{1,0:T(4,128)(2,1)}, u32[]{:S(2)}) %copy-start.10) | copy-done | bytes 1560
  26.1 22.7 %potential.1 = (bf16[512,128]{1,0:T(8,128)(2,1)S(1)}, f32[3,128]{1,0:T(4,128)S(1)}) custom-call(bf16[1,4,32,256]{3,2,1,0:T(8,128)(2,1)S(1)} %copy-done.3, s32[1,4,32,64]{3,2,1,0:T(8,128)S(1)} %copy-done.5, f32[1,4,32,64]{3,2,1,0:T(8,128)S(1)} %copy-done.7, bf16[2,2048,256]{2,1,0:T(8,128)(2,1)S(1)} %copy-done, bf16[2,256,256]{2,1,0:T(8,128)(2,1)S(1)} %copy-done.2, ...), custom_call_target="tpu_custom_call" | custom-call | flops 1000000000 | bytes 4000000 | tf_op jit(solution)/shard_map/potential/pallas_call | solution.py:395
  48.8 0.0 all-gather.2.cloned.1.call-done.w_first
  48.9 0.0 copy-done.8
  48.9 0.0 copy-done.6
  48.9 0.0 copy-done.12
  48.9 0.0 copy-done.11
  48.9 0.0 copy-start.1
  48.9 1.6 %copy-done.1 = bf16[8,128,1024]{2,1,0:T(8,128)(2,1)S(1)} copy-done((bf16[8,128,1024]{2,1,0:T(8,128)(2,1)S(1)}, bf16[8,128,1024]{2,1,0:T(8,128)(2,1)}, u32[]{:S(2)}) %copy-start.1) | copy-done | bytes 2097176
  50.5 7.6 %specialist.1 = f32[3,1,4,32]{3,2,1,0:T(4,128)} custom-call(s32[32]{0:T(128)S(1)} %bitcast.4, s32[32]{0:T(128)S(1)} %bitcast.5, s32[1]{0:T(128)} %bitcast.3.flag_count, s32[1,4,32,64]{3,2,1,0:T(8,128)S(1)} %copy-done.6, f32[1,4,32,64]{3,2,1,0:T(8,128)S(1)} %copy-done.8, bf16[512,128]{1,0:T(8,128)(2,1)S(1)} %get-tuple-element.7.planes, ...), custom_call_target="tpu_custom_call" | custom-call | flops 1000000000 | bytes 3000000 | tf_op jit(solution)/shard_map/specialist/pallas_call | solution.py:436
Async XLA Ops:
  6.5 42.3 %copy-start.8 = (f32[1,4,32,64]{3,2,1,0:T(8,128)S(1)}, f32[1,4,32,64]{3,2,1,0:T(8,128)}, u32[]{:S(2)}) copy-start(f32[1,4,32,64]{3,2,1,0:T(8,128)} %dist.3) | copy-start | bytes 98308
  6.5 42.3 %copy-start.6 = (s32[1,4,32,64]{3,2,1,0:T(8,128)S(1)}, s32[1,4,32,64]{3,2,1,0:T(8,128)}, u32[]{:S(2)}) copy-start(s32[1,4,32,64]{3,2,1,0:T(8,128)} %code.3) | copy-start | bytes 98308
  6.5 42.3 %copy-start.12 = (s32[1,1,1,32,1]{3,4,2,1,0:T(1,128)S(1)}, s32[1,1,1,32,1]{3,4,2,1,0:T(1,128)}, u32[]{:S(2)}) copy-start(s32[1,1,1,32,1]{3,4,2,1,0:T(1,128)} %param.24) | copy-start | bytes 388
  6.5 42.3 %copy-start.11 = (s32[1,1,1,32]{3,2,1,0:T(1,128)S(1)}, s32[1,1,1,32]{3,2,1,0:T(1,128)}, u32[]{:S(2)}) copy-start(s32[1,1,1,32]{3,2,1,0:T(1,128)} %param.23) | copy-start | bytes 388
  6.5 42.3 %all-gather.2.cloned.1.call-start = ((), (), s32[]{:S(2)}) async-start(), calls=%async_computation | async-start | bytes 2359296 | tf_op jit(solution)/shard_map/all_gather | solution.py:390
  18.8 1.6 %copy-start = (bf16[2,2048,256]{2,1,0:T(8,128)(2,1)S(1)}, bf16[2,2048,256]{2,1,0:T(8,128)(2,1)}, u32[]{:S(2)}) copy-start(bf16[2,2048,256]{2,1,0:T(8,128)(2,1)} %wm_hbm.1) | copy-start | bytes 6291460
  20.4 0.9 %copy-start.2 = (bf16[2,256,256]{2,1,0:T(8,128)(2,1)S(1)}, bf16[2,256,256]{2,1,0:T(8,128)(2,1)}, u32[]{:S(2)}) copy-start(bf16[2,256,256]{2,1,0:T(8,128)(2,1)} %w_update.1) | copy-start | bytes 786436
  21.3 0.8 %copy-start.3 = (bf16[1,4,32,256]{3,2,1,0:T(8,128)(2,1)S(1)}, bf16[1,4,32,256]{3,2,1,0:T(8,128)(2,1)}, u32[]{:S(2)}) copy-start(bf16[1,4,32,256]{3,2,1,0:T(8,128)(2,1)} %feat.1) | copy-start | bytes 196612
  22.2 0.8 %copy-start.4 = (bf16[256,128]{1,0:T(8,128)(2,1)S(1)}, bf16[256,128]{1,0:T(8,128)(2,1)}, u32[]{:S(2)}) copy-start(bf16[256,128]{1,0:T(8,128)(2,1)} %w_env.1) | copy-start | bytes 196612
  23.0 0.8 %copy-start.5 = (s32[1,4,32,64]{3,2,1,0:T(8,128)S(1)}, s32[1,4,32,64]{3,2,1,0:T(8,128)}, u32[]{:S(2)}) copy-start(s32[1,4,32,64]{3,2,1,0:T(8,128)} %code.3) | copy-start | bytes 98308
  23.9 0.8 %copy-start.7 = (f32[1,4,32,64]{3,2,1,0:T(8,128)S(1)}, f32[1,4,32,64]{3,2,1,0:T(8,128)}, u32[]{:S(2)}) copy-start(f32[1,4,32,64]{3,2,1,0:T(8,128)} %dist.3) | copy-start | bytes 98308
  24.7 0.7 %copy-start.9 = (f32[2,256]{1,0:T(2,128)S(1)}, f32[2,256]{1,0:T(2,128)}, u32[]{:S(2)}) copy-start(f32[2,256]{1,0:T(2,128)} %gain.1) | copy-start | bytes 6148
  25.4 0.7 %copy-start.10 = (bf16[3,256]{1,0:T(4,128)(2,1)S(1)}, bf16[3,256]{1,0:T(4,128)(2,1)}, u32[]{:S(2)}) copy-start(bf16[3,256]{1,0:T(4,128)(2,1)} %w_out.1) | copy-start | bytes 4612
  48.9 1.6 %copy-start.1 = (bf16[8,128,1024]{2,1,0:T(8,128)(2,1)S(1)}, bf16[8,128,1024]{2,1,0:T(8,128)(2,1)}, u32[]{:S(2)}) copy-start(bf16[8,128,1024]{2,1,0:T(8,128)(2,1)} %all-gather.2.cloned.1.call-done.w_first) | copy-start | bytes 6291460
Sparse Core Ops, SparseCore 0:
  9.3 34.1 all-gather.1

commit v2 on v1

--- a/solution.py
+++ b/solution.py
@@ -76,18 +76,30 @@
     return jnp.where(good, oy * 3 + oz, -1)
 
 
-def potential_kernel(
+def force_kernel(
     sizes,
+    inside,
+    flag_ids,
+    owner,
+    flag_count,
+    feat_hbm,
+    code_hbm,
+    dist_hbm,
+    wm_hbm,
+    wu_hbm,
+    w_env_hbm,
+    first_hbm,
+    gain,
+    w_out,
+    head,
+    out,
     feat,
     code,
     dist,
-    wm_hbm,
+    wm,
     w_update,
-    gain,
     w_env,
-    w_out,
-    planes_out,
-    base_out,
+    models,
     weights,
     slots,
     dcode,
@@ -100,10 +112,15 @@
     packs_proj,
     state_ref,
     proj_ref,
-    wm,
+    cand_ref,
+    dense_rows,
+    picked,
+    environ,
     send_sem,
     recv_sem,
-    wm_sem,
+    model_send,
+    model_recv,
+    load_sem,
 ):
     n_gx, n_gy, n_gz = sizes
     buffer_of = plane_buffers(n_gx)
@@ -126,6 +143,32 @@
         else:
             pl.when(me[2] > 0)(act)
 
+    def load(index, source, held):
+        copy = pltpu.make_async_copy(source, held, load_sem.at[index])
+        copy.start()
+        return copy
+
+    loads = [
+        load(index, source, held)
+        for index, (source, held) in enumerate(
+            ((feat_hbm, feat), (code_hbm, code), (dist_hbm, dist))
+        )
+    ]
+    mine = me[0] * n_gy + me[1]
+    if inside:
+        first_load = load(3, first_hbm.at[0], models.at[mine, pl.ds(0, 128)])
+    else:
+        first_load = load(3, first_hbm, models)
+    late_loads = [
+        load(4 + index, source, held)
+        for index, (source, held) in enumerate(
+            ((wm_hbm, wm), (wu_hbm, w_update), (w_env_hbm, w_env))
+        )
+    ]
+    if inside:
+        models[pl.ds(mine, 1), 128:144, :] = jnp.zeros((1, 16, models.shape[-1]), BF16)
+        models[pl.ds(mine, 1), 128:131, :] = head[...]
+
     for b in range(n_buf):
         for e in range(2):
             near[e, b, 192:256, :] = jnp.zeros((64, near.shape[-1]), BF16)
@@ -141,8 +184,11 @@
 
         along_z(step[2], greet)
 
-    weight_copy = pltpu.make_async_copy(wm_hbm, wm, wm_sem)
-    weight_copy.start()
+    if inside:
+        for dx in range(2):
+            pl.semaphore_signal(
+                barrier, inc=1, device_id=target((dx, 2, 0)), device_id_type=MESH
+            )
 
     selector = face_selector()
 
@@ -192,23 +238,58 @@
         for step, copy in zip(todo, made):
             along_z(step[2], copy.wait_send)
 
+    shift_y, shift_x, sibling = (
+        (lax.rem(me[0] + 1, n_gx), me[1]),
+        (me[0], lax.rem(me[1] + 2, n_gy)),
+        (me[0], me[1] + 1 - 2 * lax.rem(me[1], 2)),
+    )
+
+    def model_copy(index, shard, rows, to):
+        part = models.at[shard[0] * n_gy + shard[1], pl.ds(*rows)]
+        return pltpu.make_async_remote_copy(
+            src_ref=part,
+            dst_ref=part,
+            send_sem=model_send.at[index],
+            recv_sem=model_recv.at[index],
+            device_id=(to[0], to[1], me[2]),
+            device_id_type=MESH,
+        )
+
+    whole_shard = (0, 144)
+    model_copies = [
+        model_copy(0, me, whole_shard, shift_y),
+        model_copy(1, me, whole_shard, shift_x),
+        model_copy(2, me, whole_shard, sibling),
+        model_copy(3, shift_x, (0, 64), shift_y),
+        model_copy(4, shift_y, (64, 80), shift_x),
+        model_copy(5, shift_y, whole_shard, sibling),
+        model_copy(6, shift_x, whole_shard, sibling),
+        model_copy(7, (shift_y[0], shift_x[1]), whole_shard, sibling),
+    ] if inside else []
+
     def pack(state):
         return jnp.dot(selector, state, preferred_element_type=F32).astype(BF16)
 
+    loads[0].wait()
     state = feat[0].reshape(128, feat.shape[-1])
     state_ref[0] = state
     packs[0] = pack(state)
     near[0, 0, 32:160, :] = state
 
     both = (n_buf) * 3
-    here = both - 1
+    here = both - 1 + (2 if inside else 0)
     up = jnp.where(me[2] < n_gz - 1, both, 0)
     down = jnp.where(me[2] > 0, both, 0)
     pl.semaphore_wait(barrier, here + up + down)
 
     first = copies(0, state_ref.at[0], packs.at[0], near.at[0], corner.at[0])
     send_all(first)
-
+    first_load.wait()
+    for copy in model_copies[:3]:
+        copy.start()
+
+    loads[1].wait()
+    loads[2].wait()
     slot_count = code.shape[-1]
     both_rows = jnp.concatenate(
         [dist[0].reshape(128, slot_count), code[0].reshape(128, slot_count).astype(F32)], axis=1
@@ -267,13 +348,19 @@
         inv_rms = lax.rsqrt(jnp.mean(residual * residual, axis=-1, keepdims=True) + 1e-06)
         return (residual * inv_rms * gain[l : l + 1, :]).astype(BF16)
 
-    weight_copy.wait()
+    for copy in late_loads:
+        copy.wait()
     receive_all(first, near.at[0], corner.at[0])
     state = layer(0, state)
     state_ref[1] = state
     packs[1] = pack(state)
     second = copies(1, state_ref.at[1], packs.at[1], near.at[1], corner.at[1])
     send_all(second)
+    if inside:
+        model_copies[0].wait_recv()
+        model_copies[1].wait_recv()
+        for copy in model_copies[3:7]:
+            copy.start()
     near[1, 0, 32:160, :] = state
     receive_all(second, near.at[1], corner.at[1])
     state = layer(1, state)
@@ -283,36 +370,14 @@
     third = copies(2, proj_ref, packs_proj, near_proj, corner_proj)
     send_all(third)
     near_proj[0, 32:160, :] = projected
-    base_out[...] = lax.dot_general(
+    if inside:
+        model_copies[3].wait_recv()
+        model_copies[4].wait_recv()
+        model_copies[7].start()
+    base = lax.dot_general(
         w_out[...], state, (((1,), (1,)), ((), ())), preferred_element_type=F32
     )
-    receive_all(third, near_proj, corner_proj)
-    planes_out[...] = near_proj[...].reshape(planes_out.shape)
-    sent_all(first)
-    sent_all(second)
-    sent_all(third)
-
-
-def specialist_kernel(
-    n_gx,
-    flag_ids,
-    owner,
-    flag_count,
-    code,
-    dist,
-    planes,
-    base,
-    w_first,
-    w_head,
-    out,
-    rows_ref,
-    cand_ref,
-    picked,
-    environ,
-):
-    buffer_of = plane_buffers(n_gx)
     flags = flag_ids.shape[0]
-    slot_count = code.shape[-1]
     codes = code[0].reshape(128, slot_count)
     atom = iota((128, slot_count), 0)
     o = lax.div(codes, M)
@@ -322,20 +387,20 @@
     oz = lax.rem(o, 3)
     col = (atom >> 5) + oy
     z = ((atom & 31) >> 2) + oz - 1
-    inside = (z >= 0) & (z <= 7)
+    within = (z >= 0) & (z <= 7)
     top = jnp.where(z > 7, 1, 0)
     side = (col == 0) | (col == 5)
     face = 192 + top * 16 + (col - 1) * 4
     edge = 224 + (top * 2 + jnp.where(col == 5, 1, 0)) * 4
-    row = jnp.where(inside, col * 32 + z * 4, jnp.where(side, edge, face)) + j
+    row = jnp.where(within, col * 32 + z * 4, jnp.where(side, edge, face)) + j
     plane = jnp.where(ox == 1, 0, jnp.where(ox == 0, buffer_of[0], buffer_of[2]))
     cand_ref[...] = (plane * ROWS + row).astype(F32)
-    rows_ref[...] = dist[0].reshape(128, slot_count)
+    dense_rows[...] = dist[0].reshape(128, slot_count)
     picked[...] = jnp.zeros((128, 128), F32)
 
     def pick(r, carry):
         q = flag_ids[r]
-        picked[pl.ds(r, 1), 0:slot_count] = rows_ref[pl.ds(q, 1), :]
+        picked[pl.ds(r, 1), 0:slot_count] = dense_rows[pl.ds(q, 1), :]
         picked[pl.ds(r, 1), slot_count : 2 * slot_count] = cand_ref[pl.ds(q, 1), :]
         return carry
 
@@ -343,28 +408,38 @@
     turned = picked[...].T
     cut = cutoff_of(turned[0:slot_count])
     cand = turned[slot_count : 2 * slot_count]
-    lanes = iota((slot_count, planes.shape[0]), 1).astype(F32)
+    receive_all(third, near_proj, corner_proj)
+    lanes = iota((slot_count, n_buf * ROWS), 1).astype(F32)
+    planes = near_proj[...].reshape(n_buf * ROWS, near_proj.shape[-1])
     for r in range(flags):
         chosen = jnp.where(cand[:, r : r + 1] == lanes, 1.0, 0.0).astype(BF16)
-        nearby = jnp.dot(chosen, planes[...], preferred_element_type=F32)
+        nearby = jnp.dot(chosen, planes, preferred_element_type=F32)
         environ[slot_count * r : slot_count * (r + 1), :] = (cut[:, r : r + 1] * nearby).astype(BF16)
 
+    if inside:
+        for copy in (model_copies[2], *model_copies[5:]):
+            copy.wait_recv()
     lane = iota(base.shape, 1)
 
     def correct(r, forces):
         p = owner[r]
         rows = environ[pl.ds(pl.multiple_of(r * slot_count, slot_count), slot_count), :]
-        wide = jnp.dot(rows, w_first[p], preferred_element_type=F32)
+        wide = jnp.dot(rows, models[p, 0:128, :], preferred_element_type=F32)
         hidden = (wide / (1.0 + jnp.exp(-wide))).astype(BF16).astype(F32)
         pooled = (jnp.sum(hidden, axis=0, keepdims=True) * (1.0 / slot_count)).astype(BF16)
-        terms = pooled.astype(F32) * w_head[p].astype(F32)
+        terms = pooled.astype(F32) * (models[p, 128:131, :] if inside else head[p]).astype(F32)
         force = jnp.sum(terms, axis=1, keepdims=True)
         live = jnp.where(r < flag_count[0], 1.0, 0.0)
         return forces + jnp.where(lane == flag_ids[r], force * live, 0.0)
 
-    forces = lax.fori_loop(0, flags, correct, base[...], unroll=4)
+    forces = lax.fori_loop(0, flags, correct, base, unroll=4)
     for y in range(out.shape[2]):
         out[:, 0, y, :] = forces[:, 32 * y : 32 * (y + 1)]
+    sent_all(first)
+    sent_all(second)
+    sent_all(third)
+    for copy in model_copies:
+        copy.wait_send()
 
 
 def per_device(
@@ -387,20 +462,35 @@
     feature_width = features.shape[-1]
     env_width = w_env.shape[-1]
     message_count = len(messages(sizes[0]))
-    all_first = lax.all_gather(w_first[0], ("gx", "gy"), axis=0)
-    all_head = lax.all_gather(w_head[0], ("gx", "gy"), axis=0)
+    local_ids = flag_ids.reshape(-1)
+    owner = flag_owner.reshape(-1)
+    flags = local_ids.shape[0]
+    slot_count = distance.shape[-1]
+    inside = sizes[:2] == (2, 4)
+    if inside:
+        models_shape = (8, 144, w_first.shape[-1])
+    else:
+        w_first = lax.all_gather(w_first[0], ("gx", "gy"), axis=0)[owner]
+        w_head = lax.all_gather(w_head[0], ("gx", "gy"), axis=0)[owner]
+        owner = jnp.arange(flags, dtype=jnp.int32)
+        models_shape = w_first.shape
 
     vmem = pl.BlockSpec(memory_space=pltpu.VMEM)
     smem = pl.BlockSpec(memory_space=pltpu.SMEM)
-    planes, base = pl.pallas_call(
-        functools.partial(potential_kernel, sizes),
-        out_shape=(
-            jax.ShapeDtypeStruct((n_buf * ROWS, env_width), BF16),
-            jax.ShapeDtypeStruct((3, 128), F32),
-        ),
-        in_specs=[vmem, vmem, vmem, pl.BlockSpec(memory_space=pl.ANY)] + [vmem] * 4,
-        out_specs=(vmem, vmem),
+    anywhere = pl.BlockSpec(memory_space=pl.ANY)
+    return pl.pallas_call(
+        functools.partial(force_kernel, sizes, inside),
+        out_shape=jax.ShapeDtypeStruct((3,) + features.shape[:3], F32),
+        in_specs=[smem] * 3 + [anywhere] * 7 + [vmem] * 3,
+        out_specs=vmem,
         scratch_shapes=[
+            pltpu.VMEM(features.shape, BF16),
+            pltpu.VMEM(neighbour_code.shape, jnp.int32),
+            pltpu.VMEM(distance.shape, F32),
+            pltpu.VMEM(w_message.shape, BF16),
+            pltpu.VMEM(w_update.shape, BF16),
+            pltpu.VMEM(w_env.shape, BF16),
+            pltpu.VMEM(models_shape, BF16),
             pltpu.VMEM((NRB * 128, n_buf * ROWS), BF16),
             pltpu.VMEM((128, 128), F32),
             pltpu.VMEM((216, 128), F32),
@@ -413,52 +503,37 @@
             pltpu.VMEM((96, env_width), BF16),
             pltpu.VMEM((2, 128, feature_width), BF16),
             pltpu.VMEM((128, env_width), BF16),
-            pltpu.VMEM(w_message.shape, BF16),
-            pltpu.SemaphoreType.DMA((3, message_count)),
-            pltpu.SemaphoreType.DMA((3, message_count)),
-            pltpu.SemaphoreType.DMA,
-        ],
-        compiler_params=pltpu.CompilerParams(
-            collective_id=0, has_side_effects=True, vmem_limit_bytes=32 * 1024 * 1024
-        ),
-        cost_estimate=pl.CostEstimate(flops=10**9, bytes_accessed=4 * 10**6, transcendentals=10**6),
-        name="potential",
-    )(features, neighbour_code, distance, w_message, w_update, norm_gain, w_env, w_out)
-
-    owner = flag_owner.reshape(-1)
-    if all_first.shape[0] > 8:
-        all_first = all_first[owner]
-        all_head = all_head[owner]
-        owner = jnp.arange(owner.shape[0], dtype=jnp.int32)
-    local_ids = flag_ids.reshape(-1)
-    flags = local_ids.shape[0]
-    slot_count = distance.shape[-1]
-    return pl.pallas_call(
-        functools.partial(specialist_kernel, sizes[0]),
-        out_shape=jax.ShapeDtypeStruct((3,) + features.shape[:3], F32),
-        in_specs=[smem] * 3 + [vmem] * 6,
-        out_specs=vmem,
-        scratch_shapes=[
             pltpu.VMEM((128, slot_count), F32),
             pltpu.VMEM((128, slot_count), F32),
             pltpu.VMEM((128, 128), F32),
             pltpu.VMEM((flags * slot_count, env_width), BF16),
+            pltpu.SemaphoreType.DMA((3, message_count)),
+            pltpu.SemaphoreType.DMA((3, message_count)),
+            pltpu.SemaphoreType.DMA((8,)),
+            pltpu.SemaphoreType.DMA((8,)),
+            pltpu.SemaphoreType.DMA((7,)),
         ],
-        compiler_params=pltpu.CompilerParams(vmem_limit_bytes=40 * 1024 * 1024),
+        compiler_params=pltpu.CompilerParams(
+            collective_id=0, has_side_effects=True, vmem_limit_bytes=56 * 1024 * 1024
+        ),
         cost_estimate=pl.CostEstimate(
-            flops=10**9, bytes_accessed=3 * 10**6, transcendentals=2 * 10**6
+            flops=2 * 10**9, bytes_accessed=4 * 10**6, transcendentals=3 * 10**6
         ),
-        name="specialist",
+        name="forces",
     )(
         local_ids,
         owner,
         flag_count.reshape(-1),
+        features,
         neighbour_code,
         distance,
-        planes,
-        base,
-        all_first,
-        all_head,
+        w_message,
+        w_update,
+        w_env,
+        w_first,
+        norm_gain,
+        w_out,
+        w_head,
     )
 
 

time: 65.4 us -> 35.3 us (0.54)
  between operations: 14.1 us -> 0.66 us
  blocking collectives: 10.8 us -> 0 us
  local copies, waits for them, and re-layouts: 8.91 us -> 1.29 us
  Pallas kernels: 30.3 us -> 33.1 us
  waiting for transfers between devices: 0.7 us -> 0 us
    all_gather x1 -> x0, blocking collectives: 10.8 us -> none  [per_device(): all_head = lax.all_gather(w_head[0], ('gx', 'gy'), axis=0)]
    unnamed x26 -> x1, local copies, waits for them, and re-layouts: 8.91 us -> 1.29 us
    pallas_call x2 -> x1, Pallas kernels: 30.3 us -> 33.1 us  [per_device(): pl.pallas_call(functools.partial(force_kernel, sizes, inside), out_shape=...]
    unnamed x1 -> x0, waiting for transfers between devices: 0.68 us -> none
  transfers between devices with their start and end apart: 1 -> 0, of which waited for: 0 -> 0; matrix products, arithmetic and copies ran while one was open for 0% -> 0% of each run, Pallas kernels for 35% -> 0%
where the time goes in v2:
time: 35.3 us; the launch traced here: 35 us
  Pallas kernels  33.1 us (94%)
  local copies, waits for them, and re-layouts  1.29 us (4%)
  between operations  0.66 us (2%)
    pallas_call x1, Pallas kernels, per_device(): pl.pallas_call(functools.partial(force_kernel, sizes, inside), out_shape=...  33.1 us
    unnamed x1, local copies, waits for them, and re-layouts  1.29 us

profile of v2, /device:TPU:0, one launch (start us, length us, event | category | flops | bytes accessed | tf_op | source)
XLA Modules:
  0.0 35.0 jit_solution(7698946353768818876)
XLA Ops:
  0.7 33.1 %forces.1 = f32[3,1,4,32]{3,2,1,0:T(4,128)} custom-call(s32[32]{0:T(128)} %bitcast.4, s32[32]{0:T(128)} %bitcast.5, s32[1]{0:T(128)} %bitcast.3.flag_count, bf16[1,4,32,256]{3,2,1,0:T(8,128)(2,1)} %feat_hbm.1, s32[1,4,32,64]{3,2,1,0:T(8,128)} %code_hbm.1, f32[1,4,32,64]{3,2,1,0:T(8,128)} %dist_hbm.1, bf16[2,2048,256]{2,1,0:T(8,128)(2,1)} %wm_hbm.1, ...), custom_call_target="tpu_custom_call" | custom-call | flops 2000000000 | bytes 4000000 | tf_op jit(solution)/shard_map/forces/pallas_call | solution.py:481
  33.8 1.3 %copy.16 = f32[3,1,4,32]{3,2,1,0:T(4,128)} copy(f32[3,1,4,32]{3,2,1,0:T(4,128)} %forces.1) | data formatting | bytes 3072

commit v3 on v2

--- a/solution.py
+++ b/solution.py
@@ -116,6 +116,7 @@
     dense_rows,
     picked,
     environ,
+    chosen,
     send_sem,
     recv_sem,
     model_send,
@@ -335,15 +336,10 @@
     def layer(l, state):
         width = state.shape[-1]
         rows = near[l].reshape(n_buf * ROWS, width)
-        message = jnp.zeros((128, width), F32)
-        for k in range(NRB):
-            summed = jnp.dot(weights[128 * k : 128 * (k + 1), :], rows, preferred_element_type=F32)
-            message = message + jnp.dot(
-                summed.astype(BF16),
-                wm[l, width * k : width * (k + 1), :],
-                preferred_element_type=F32,
-            )
-        active = (message / (1.0 + jnp.exp(-message))).astype(BF16)
+        summed = jnp.dot(weights[...], rows, preferred_element_type=F32).astype(BF16)
+        summed = jnp.concatenate([summed[128 * k : 128 * (k + 1)] for k in range(NRB)], axis=1)
+        half = 0.5 * jnp.dot(summed, wm[l], preferred_element_type=F32)
+        active = (half + half * jnp.tanh(half)).astype(BF16)
         residual = state.astype(F32) + jnp.dot(active, w_update[l], preferred_element_type=F32)
         inv_rms = lax.rsqrt(jnp.mean(residual * residual, axis=-1, keepdims=True) + 1e-06)
         return (residual * inv_rms * gain[l : l + 1, :]).astype(BF16)
@@ -356,27 +352,7 @@
     packs[1] = pack(state)
     second = copies(1, state_ref.at[1], packs.at[1], near.at[1], corner.at[1])
     send_all(second)
-    if inside:
-        model_copies[0].wait_recv()
-        model_copies[1].wait_recv()
-        for copy in model_copies[3:7]:
-            copy.start()
     near[1, 0, 32:160, :] = state
-    receive_all(second, near.at[1], corner.at[1])
-    state = layer(1, state)
-    projected = jnp.dot(state, w_env[...], preferred_element_type=F32).astype(BF16)
-    proj_ref[...] = projected
-    packs_proj[...] = pack(projected)
-    third = copies(2, proj_ref, packs_proj, near_proj, corner_proj)
-    send_all(third)
-    near_proj[0, 32:160, :] = projected
-    if inside:
-        model_copies[3].wait_recv()
-        model_copies[4].wait_recv()
-        model_copies[7].start()
-    base = lax.dot_general(
-        w_out[...], state, (((1,), (1,)), ((), ())), preferred_element_type=F32
-    )
     flags = flag_ids.shape[0]
     codes = code[0].reshape(128, slot_count)
     atom = iota((128, slot_count), 0)
@@ -406,15 +382,43 @@
 
     lax.fori_loop(0, flags, pick, 0, unroll=8)
     turned = picked[...].T
-    cut = cutoff_of(turned[0:slot_count])
+    half_cut = 0.5 * cutoff_of(turned[0:slot_count])
     cand = turned[slot_count : 2 * slot_count]
+    lanes = iota((slot_count, n_buf * ROWS), 1).astype(F32)
+    for r in range(flags):
+        chosen[slot_count * r : slot_count * (r + 1), :] = jnp.where(
+            cand[:, r : r + 1] == lanes, 1.0, 0.0
+        ).astype(BF16)
+    if inside:
+        model_copies[0].wait_recv()
+        model_copies[1].wait_recv()
+        for copy in model_copies[3:7]:
+            copy.start()
+    receive_all(second, near.at[1], corner.at[1])
+    state = layer(1, state)
+    projected = jnp.dot(state, w_env[...], preferred_element_type=F32).astype(BF16)
+    proj_ref[...] = projected
+    packs_proj[...] = pack(projected)
+    third = copies(2, proj_ref, packs_proj, near_proj, corner_proj)
+    send_all(third)
+    near_proj[0, 32:160, :] = projected
+    if inside:
+        model_copies[3].wait_recv()
+        model_copies[4].wait_recv()
+        model_copies[7].start()
+    base = lax.dot_general(
+        w_out[...], state, (((1,), (1,)), ((), ())), preferred_element_type=F32
+    )
     receive_all(third, near_proj, corner_proj)
-    lanes = iota((slot_count, n_buf * ROWS), 1).astype(F32)
     planes = near_proj[...].reshape(n_buf * ROWS, near_proj.shape[-1])
-    for r in range(flags):
-        chosen = jnp.where(cand[:, r : r + 1] == lanes, 1.0, 0.0).astype(BF16)
-        nearby = jnp.dot(chosen, planes, preferred_element_type=F32)
-        environ[slot_count * r : slot_count * (r + 1), :] = (cut[:, r : r + 1] * nearby).astype(BF16)
+    for r0 in range(0, flags, 8):
+        nearby = jnp.dot(
+            chosen[slot_count * r0 : slot_count * (r0 + 8), :], planes, preferred_element_type=F32
+        )
+        for r in range(r0, r0 + 8):
+            environ[slot_count * r : slot_count * (r + 1), :] = (
+                half_cut[:, r : r + 1] * nearby[slot_count * (r - r0) : slot_count * (r - r0 + 1)]
+            ).astype(BF16)
 
     if inside:
         for copy in (model_copies[2], *model_copies[5:]):
@@ -424,15 +428,15 @@
     def correct(r, forces):
         p = owner[r]
         rows = environ[pl.ds(pl.multiple_of(r * slot_count, slot_count), slot_count), :]
-        wide = jnp.dot(rows, models[p, 0:128, :], preferred_element_type=F32)
-        hidden = (wide / (1.0 + jnp.exp(-wide))).astype(BF16).astype(F32)
+        half = jnp.dot(rows, models[p, 0:128, :], preferred_element_type=F32)
+        hidden = half + half * jnp.tanh(half)
         pooled = (jnp.sum(hidden, axis=0, keepdims=True) * (1.0 / slot_count)).astype(BF16)
         terms = pooled.astype(F32) * (models[p, 128:131, :] if inside else head[p]).astype(F32)
         force = jnp.sum(terms, axis=1, keepdims=True)
         live = jnp.where(r < flag_count[0], 1.0, 0.0)
         return forces + jnp.where(lane == flag_ids[r], force * live, 0.0)
 
-    forces = lax.fori_loop(0, flags, correct, base, unroll=4)
+    forces = lax.fori_loop(0, flags, correct, base, unroll=8)
     for y in range(out.shape[2]):
         out[:, 0, y, :] = forces[:, 32 * y : 32 * (y + 1)]
     sent_all(first)
@@ -507,6 +511,7 @@
             pltpu.VMEM((128, slot_count), F32),
             pltpu.VMEM((128, 128), F32),
             pltpu.VMEM((flags * slot_count, env_width), BF16),
+            pltpu.VMEM((flags * slot_count, n_buf * ROWS), BF16),
             pltpu.SemaphoreType.DMA((3, message_count)),
             pltpu.SemaphoreType.DMA((3, message_count)),
             pltpu.SemaphoreType.DMA((8,)),

time: 35.3 us -> 33.2 us (0.941)
  Pallas kernels: 33.1 us -> 31.1 us
    pallas_call x1, Pallas kernels: 33.1 us -> 31.1 us  [per_device(): pl.pallas_call(functools.partial(force_kernel, sizes, inside), out_shape=...]
where the time goes in v3:
time: 33.2 us; the launch traced here: 33 us
  Pallas kernels  31.1 us (94%)
  local copies, waits for them, and re-layouts  1.29 us (4%)
  between operations  0.66 us (2%)
    pallas_call x1, Pallas kernels, per_device(): pl.pallas_call(functools.partial(force_kernel, sizes, inside), out_shape=...  31.1 us
    unnamed x1, local copies, waits for them, and re-layouts  1.29 us

profile of v3, /device:TPU:0, one launch (start us, length us, event | category | flops | bytes accessed | tf_op | source)
XLA Modules:
  0.0 33.0 jit_solution(4946792515758772614)
XLA Ops:
  0.7 31.1 %forces.1 = f32[3,1,4,32]{3,2,1,0:T(4,128)} custom-call(s32[32]{0:T(128)} %bitcast.4, s32[32]{0:T(128)} %bitcast.5, s32[1]{0:T(128)} %bitcast.3.flag_count, bf16[1,4,32,256]{3,2,1,0:T(8,128)(2,1)} %feat_hbm.1, s32[1,4,32,64]{3,2,1,0:T(8,128)} %code_hbm.1, f32[1,4,32,64]{3,2,1,0:T(8,128)} %dist_hbm.1, bf16[2,2048,256]{2,1,0:T(8,128)(2,1)} %wm_hbm.1, ...), custom_call_target="tpu_custom_call" | custom-call | flops 2000000000 | bytes 4000000 | tf_op jit(solution)/shard_map/forces/pallas_call | solution.py:485
  31.7 1.3 %copy.16 = f32[3,1,4,32]{3,2,1,0:T(4,128)} copy(f32[3,1,4,32]{3,2,1,0:T(4,128)} %forces.1) | data formatting | bytes 3072

commit v4 on v3

--- a/solution.py
+++ b/solution.py
@@ -25,7 +25,7 @@
 
 
 def messages(n_gx):
-    steps_x = (0, 1) if n_gx == 2 else (0, 1, -1)
+    steps_x = (1, 0) if n_gx == 2 else (1, -1, 0)
     return [
         (dx, dy, dz)
         for dx in steps_x
@@ -226,14 +226,14 @@
         for step, copy in zip(todo, made):
             along_z(step[2], copy.start)
 
-    def receive_all(made, plane, corners):
+    def receive(made, plane, corners, b):
         for step, copy in zip(todo, made):
-            along_z(-step[2], copy.wait_recv)
-        for b in range(n_buf):
-            tile = corners[b, 0].astype(F32)
-            for g in range(1, 4):
-                tile = tile + corners[b, g].astype(F32)
-            plane[b, 224:240, :] = tile.astype(BF16)
+            if (0 if step[0] == 0 else buffer_of[0 if step[0] > 0 else 2]) == b:
+                along_z(-step[2], copy.wait_recv)
+        tile = corners[b, 0].astype(F32)
+        for g in range(1, 4):
+            tile = tile + corners[b, g].astype(F32)
+        plane[b, 224:240, :] = tile.astype(BF16)
 
     def sent_all(made):
         for step, copy in zip(todo, made):
@@ -333,10 +333,15 @@
                     total.astype(BF16)
                 )
 
-    def layer(l, state):
+    def layer(l, state, made):
         width = state.shape[-1]
-        rows = near[l].reshape(n_buf * ROWS, width)
-        summed = jnp.dot(weights[...], rows, preferred_element_type=F32).astype(BF16)
+        summed = jnp.zeros((NRB * 128, width), F32)
+        for b in range(n_buf):
+            receive(made, near.at[l], corner.at[l], b)
+            summed = summed + jnp.dot(
+                weights[:, ROWS * b : ROWS * (b + 1)], near[l, b], preferred_element_type=F32
+            )
+        summed = summed.astype(BF16)
         summed = jnp.concatenate([summed[128 * k : 128 * (k + 1)] for k in range(NRB)], axis=1)
         half = 0.5 * jnp.dot(summed, wm[l], preferred_element_type=F32)
         active = (half + half * jnp.tanh(half)).astype(BF16)
@@ -346,8 +351,7 @@
 
     for copy in late_loads:
         copy.wait()
-    receive_all(first, near.at[0], corner.at[0])
-    state = layer(0, state)
+    state = layer(0, state, first)
     state_ref[1] = state
     packs[1] = pack(state)
     second = copies(1, state_ref.at[1], packs.at[1], near.at[1], corner.at[1])
@@ -394,8 +398,7 @@
         model_copies[1].wait_recv()
         for copy in model_copies[3:7]:
             copy.start()
-    receive_all(second, near.at[1], corner.at[1])
-    state = layer(1, state)
+    state = layer(1, state, second)
     projected = jnp.dot(state, w_env[...], preferred_element_type=F32).astype(BF16)
     proj_ref[...] = projected
     packs_proj[...] = pack(projected)
@@ -409,7 +412,8 @@
     base = lax.dot_general(
         w_out[...], state, (((1,), (1,)), ((), ())), preferred_element_type=F32
     )
-    receive_all(third, near_proj, corner_proj)
+    for b in range(n_buf):
+        receive(third, near_proj, corner_proj, b)
     planes = near_proj[...].reshape(n_buf * ROWS, near_proj.shape[-1])
     for r0 in range(0, flags, 8):
         nearby = jnp.dot(

time: 33.2 us -> 32.9 us (level)
  no operation moved by 1% of the time
where the time goes in v4:
time: 32.9 us; the launch traced here: 32.7 us
  Pallas kernels  30.8 us (94%)
  local copies, waits for them, and re-layouts  1.29 us (4%)
  between operations  0.66 us (2%)
    pallas_call x1, Pallas kernels, per_device(): pl.pallas_call(functools.partial(force_kernel, sizes, inside), out_shape=...  30.8 us
    unnamed x1, local copies, waits for them, and re-layouts  1.29 us

profile of v4, /device:TPU:0, one launch (start us, length us, event | category | flops | bytes accessed | tf_op | source)
XLA Modules:
  0.0 32.7 jit_solution(4032630261348658613)
XLA Ops:
  0.7 30.8 %forces.1 = f32[3,1,4,32]{3,2,1,0:T(4,128)} custom-call(s32[32]{0:T(128)} %bitcast.4, s32[32]{0:T(128)} %bitcast.5, s32[1]{0:T(128)} %bitcast.3.flag_count, bf16[1,4,32,256]{3,2,1,0:T(8,128)(2,1)} %feat_hbm.1, s32[1,4,32,64]{3,2,1,0:T(8,128)} %code_hbm.1, f32[1,4,32,64]{3,2,1,0:T(8,128)} %dist_hbm.1, bf16[2,2048,256]{2,1,0:T(8,128)(2,1)} %wm_hbm.1, ...), custom_call_target="tpu_custom_call" | custom-call | flops 2000000000 | bytes 4000000 | tf_op jit(solution)/shard_map/forces/pallas_call | solution.py:489
  31.4 1.3 %copy.16 = f32[3,1,4,32]{3,2,1,0:T(4,128)} copy(f32[3,1,4,32]{3,2,1,0:T(4,128)} %forces.1) | data formatting | bytes 3072
